TPU v7x, 32 devices: a whole 2x2x4 slice. The times are simulated.
32 devices in a mesh: groups: 2 (over y), feat: 4 (over z), dp: 4 (over x, core).
Axes of the slice: x: 2, y: 2, z: 4, core: 2. Of those that a mesh axis runs over, the one named last changes fastest.
Arguments:
- features: bfloat16 [2048, 8192], P(('groups', 'dp'), 'feat'), parts along dimension 0, may hold values from -6 to 6
- bn_gain: float32 [8192], P('feat'), may hold values from 0.1 to 1.9
- bn_shift: float32 [8192], P('feat'), may hold values from -0.5 to 0.5
- weight: bfloat16 [8192, 8192], P('feat'), may hold values from -2 to 2
Outputs:
- covariance: float32 [16384, 8192], P(('groups', 'dp'), 'feat'), parts along dimension 0
- grad_in: bfloat16 [2048, 8192], P(('groups', 'dp'), 'feat'), parts along dimension 0
There are 2 independent parts, one for each index of `groups`. A program takes and returns all parts, laid end to end along the dimension named above; an argument that names none is the same for every part. Nothing has to cross between parts.
All inputs are finite; a program needn't handle non-finite values.
Results may differ from a plain program's by a relative error of at most 0.014.
Values may be sent and summed in bfloat16 or wider, within the bound.
A program may use at most 256 MiB of HBM per device.

v0:
```python
import jax
import jax.numpy as jnp
from jax import lax
from jax.sharding import PartitionSpec as P


def whole_rows(centered):
    return lax.all_gather(centered, "feat", axis=1, tiled=True)


def shards(features, bn_gain, bn_shift, weight):
    dp_count = lax.axis_size("dp")
    feat_count = lax.axis_size("feat")
    local_rows = features.shape[0]
    images = local_rows * dp_count
    hidden = features.astype(jnp.float32)
    col_sums, col_squares = lax.psum((jnp.sum(hidden, 0), jnp.sum(hidden * hidden, 0)), "dp")
    mean_h = col_sums / images
    var_h = col_squares / images - mean_h * mean_h
    normed = (hidden - mean_h) * lax.rsqrt(var_h + 1e-05) * bn_gain + bn_shift
    activated = jnp.maximum(normed, 0.0).astype(jnp.bfloat16)
    partial_value = jnp.dot(activated, weight, preferred_element_type=jnp.float32)
    projected = lax.psum_scatter(partial_value, "feat", scatter_dimension=1, tiled=True).astype(
        jnp.bfloat16
    )
    proj_f = projected.astype(jnp.float32)
    proj_mean = lax.psum(jnp.sum(proj_f, 0), "dp") / images
    centered = (proj_f - proj_mean).astype(jnp.bfloat16)
    cent_f = centered.astype(jnp.float32)
    width_f = centered.shape[1]
    width_x = width_f * feat_count // dp_count
    cent_full = None
    cent_full = whole_rows(centered)
    cent_x = lax.all_to_all(cent_full, "dp", split_axis=1, concat_axis=0, tiled=True)
    piece = lax.all_gather(centered, "dp", axis=0, tiled=True)
    cov_tile = lax.dot_general(
        cent_x, piece, (((0,), (0,)), ((), ())), preferred_element_type=jnp.float32
    )
    piece_f = piece.astype(jnp.float32)
    cov_tile, sq_sum = (cov_tile, jnp.sum(piece_f * piece_f, 0))
    covariance = cov_tile / (images - 1)
    proj_var = sq_sum / (images - 1)
    spread = jnp.sqrt(proj_var + 0.0001)
    row_ids = lax.axis_index("dp") * width_x + jnp.arange(width_x, dtype=jnp.int32)[:, None]
    col_ids = lax.axis_index("feat") * width_f + jnp.arange(width_f, dtype=jnp.int32)[None, :]
    off_diag = jnp.where(row_ids == col_ids, 0.0, covariance).astype(jnp.bfloat16)
    mixed = jnp.dot(
        cent_full,
        lax.all_gather(off_diag, "dp", axis=0, tiled=True),
        preferred_element_type=jnp.float32,
    )
    scale_up = images / (images - 1)
    active = jnp.where(spread < 1.0, 1.0 / spread, 0.0)
    grad_proj = (4.0 * scale_up * mixed - 25.0 * scale_up * active * cent_f).astype(jnp.bfloat16)
    grad_in = lax.dot_general(
        lax.all_gather(grad_proj, "feat", axis=1, tiled=True),
        weight,
        (((1,), (1,)), ((), ())),
        preferred_element_type=jnp.float32,
    )
    return (covariance, grad_in.astype(jnp.bfloat16))


def solution(mesh):
    in_specs = (P(("groups", "dp"), "feat"), P("feat"), P("feat"), P("feat", None))
    out_specs = (P(("groups", "dp"), "feat"), P(("groups", "dp"), "feat"))
    return jax.shard_map(shards, mesh=mesh, in_specs=in_specs, out_specs=out_specs, check_vma=False)
```

profile of v0, /device:TPU:0, one launch (start us, length us, event | category | flops | bytes accessed | tf_op | source)
XLA Modules:
  0.0 694.4 jit_solution(14080801374418411626)
XLA Ops:
  7.2 0.0 reduce-scatter.2.cloned.1.call-start
  7.2 1.5 convert_reduce_fusion
  8.7 12.7 %all-reduce = (f32[2048]{0:T(1024)S(1)}, f32[2048]{0:T(1024)S(1)}) all-reduce(f32[2048]{0:T(1024)S(1)} %get-tuple-element.3, f32[2048]{0:T(1024)S(1)} %get-tuple-element.2), channel_id=1, replica_groups=mesh['groups'=2,'feat'=4,'dp'=4] {'dp'}, use_global_device_ids=true, to_apply=%region_3.0 | all-reduce | flops 4096 | bytes 32768 | tf_op jit(solution)/shard_map/psum | solution.py:17
  21.4 17.4 %fusion.9 = f32[256,8192]{1,0:T(8,128)} fusion(bf16[2048,8192]{1,0:T(8,128)(2,1)} %param.7, bf16[256,2048]{1,0:T(8,128)(2,1)} %param.4, f32[2048]{0:T(1024)} %param.6, f32[2048]{0:T(1024)} %param.5, f32[2048]{0:T(1024)S(1)} %get-tuple-element.7, f32[2048]{0:T(1024)S(1)} %get-tuple-element.6), kind=kOutput, calls=%fused_computation.20 | convolution fusion | flops 8593604608 | bytes 43024384 | tf_op jit(solution)/shard_map/dot_general | solution.py:22
  38.8 0.0 reduce-scatter.2.cloned.1.call-update
  38.9 0.0 all-gather.5.cloned.1.call-start
  38.9 144.9 %reduce-scatter.2.cloned.1.call-done = f32[256,2048]{1,0:T(8,128)} async-done(((f32[256,8192]{1,0:T(8,128)}), f32[256,2048]{1,0:T(8,128)}) %reduce-scatter.2.cloned.1.call-update) | async-done | bytes 2097168 | tf_op jit(solution)/shard_map/reduce_scatter | solution.py:23
  183.8 1.7 convert_reduce_fusion.1
  185.5 6.5 psum.23
  192.0 2.7 fusion.2
  194.8 0.0 all-gather.5.cloned.1.call-update
  194.8 0.0 all-gather.7.cloned.1.call-start
  194.9 0.7 all-gather.7.cloned.1.call-update
  195.6 80.5 %all-gather.5.cloned.1.call-done = bf16[256,8192]{1,0:T(8,128)(2,1)} async-done(((bf16[256,2048]{1,0:T(8,128)(2,1)}), bf16[256,8192]{1,0:T(8,128)(2,1)}) %all-gather.5.cloned.1.call-update) | async-done | bytes 4194320 | tf_op jit(solution)/shard_map/all_gather | solution.py:8
  276.0 4.8 copy.9
  280.8 4.9 all-to-all-start
  285.8 0.0 all-gather.9.cloned.1.call-start
  285.8 46.1 %all-gather.7.cloned.1.call-done = bf16[1024,2048]{1,0:T(8,128)(2,1)} async-done(((bf16[256,2048]{1,0:T(8,128)(2,1)}), bf16[1024,2048]{1,0:T(8,128)(2,1)}) %all-gather.7.cloned.1.call-update) | async-done | bytes 4194320 | tf_op jit(solution)/shard_map/all_gather | solution.py:35
  332.0 22.7 %all-to-all-done = bf16[256,4,2048]{2,0,1:T(8,128)(2,1)} async-done(((bf16[256,4,2048]{2,0,1:T(8,128)(2,1)}), bf16[256,4,2048]{2,0,1:T(8,128)(2,1)}, u32[]{:S(2)}, u32[]{:S(2)}) %all-to-all-start) | async-done | bytes 4194336 | tf_op jit(solution)/shard_map/all_to_all | solution.py:34
  354.6 17.6 %select_convert_fusion = (bf16[2048,2048]{1,0:T(8,128)(2,1)}, f32[2048,2048]{1,0:T(8,128)}) fusion(s32[2048]{0:T(1024)S(1)} %get-tuple-element.10, s32[2048]{0:T(1024)S(1)} %get-tuple-element.11, bf16[1024,2048]{1,0:T(8,128)(2,1)} %bitcast.1, bf16[1024,2048]{1,0:T(8,128)(2,1)} %all-gather.7.cloned.1.call-done), kind=kOutput, calls=%fused_computation | convolution fusion | flops 8602517504 | bytes 33570816 | tf_op jit(solution)/shard_map/dot_general | solution.py:36
  372.3 0.0 all-gather.9.cloned.1.call-update
  372.3 0.0 copy-start
  372.3 0.2 all-gather.11.cloned.1.call-start
  372.5 3.1 multiply_reduce_fusion
  375.7 197.5 %all-gather.9.cloned.1.call-done = bf16[8192,2048]{1,0:T(8,128)(2,1)} async-done(((bf16[2048,2048]{1,0:T(8,128)(2,1)}), bf16[8192,2048]{1,0:T(8,128)(2,1)}) %all-gather.9.cloned.1.call-update) | async-done | bytes 33554448 | tf_op jit(solution)/shard_map/all_gather | solution.py:49
  573.2 0.0 copy-done
  573.2 17.0 %fusion.1 = bf16[256,2048]{1,0:T(8,128)(2,1)} fusion(bf16[256,8192]{1,0:T(8,128)(2,1)} %all-gather.5.cloned.1.call-done, bf16[8192,2048]{1,0:T(8,128)(2,1)} %all-gather.9.cloned.1.call-done, bf16[256,2048]{1,0:T(8,128)(2,1)S(1)} %copy-done, f32[2048]{0:T(1024)S(1)} %select_multiply_fusion), kind=kOutput, calls=%fused_computation.11 | convolution fusion | flops 8592556032 | bytes 39854080 | tf_op jit(solution)/shard_map/dot_general | solution.py:47
  590.2 0.0 all-gather.11.cloned.1.call-update
  590.3 80.9 %all-gather.11.cloned.1.call-done = bf16[256,8192]{1,0:T(8,128)(2,1)} async-done(((bf16[256,2048]{1,0:T(8,128)(2,1)}), bf16[256,8192]{1,0:T(8,128)(2,1)}) %all-gather.11.cloned.1.call-update) | async-done | bytes 4194320 | tf_op jit(solution)/shard_map/all_gather | solution.py:56
  671.2 16.6 %convolution_convert_fusion = bf16[256,2048]{1,0:T(8,128)(2,1)} fusion(bf16[256,8192]{1,0:T(8,128)(2,1)} %all-gather.11.cloned.1.call-done, bf16[2048,8192]{1,0:T(8,128)(2,1)} %param.7), kind=kOutput, calls=%fused_computation.12 | convolution fusion | flops 8590458880 | bytes 38797312 | tf_op jit(solution)/shard_map/dot_general | solution.py:55
  (4 shorter events, 0.0 us)
Async XLA Ops:
  7.2 176.7 %reduce-scatter.2.cloned.1.call-start = ((), (), s32[]{:S(2)}) async-start(), calls=%async_computation.2 | async-start | bytes 10485760 | tf_op jit(solution)/shard_map/reduce_scatter | solution.py:23
  38.9 237.2 %all-gather.5.cloned.1.call-start = ((), (), s32[]{:S(2)}) async-start(), calls=%async_computation.3 | async-start | bytes 5242880 | tf_op jit(solution)/shard_map/all_gather | solution.py:8
  194.8 137.1 %all-gather.7.cloned.1.call-start = ((), (), s32[]{:S(2)}) async-start(), calls=%async_computation.4 | async-start | bytes 5242880 | tf_op jit(solution)/shard_map/all_gather | solution.py:35
  280.8 73.8 %all-to-all-start = ((bf16[256,4,2048]{2,0,1:T(8,128)(2,1)}), bf16[256,4,2048]{2,0,1:T(8,128)(2,1)}, u32[]{:S(2)}, u32[]{:S(2)}) async-start(bf16[256,4,2048]{2,0,1:T(8,128)(2,1)} %bitcast.14), calls=%async_computation.1 | async-start | bytes 8388608 | tf_op jit(solution)/shard_map/all_to_all | solution.py:34
  285.8 287.4 %all-gather.9.cloned.1.call-start = ((), (), s32[]{:S(2)}) async-start(), calls=%async_computation.5 | async-start | bytes 41943040 | tf_op jit(solution)/shard_map/all_gather | solution.py:49
  372.3 200.9 %copy-start = (bf16[256,2048]{1,0:T(8,128)(2,1)S(1)}, bf16[256,2048]{1,0:T(8,128)(2,1)}, u32[]{:S(2)}) copy-start(bf16[256,2048]{1,0:T(8,128)(2,1)} %fusion.2) | copy-start | bytes 3145732
  372.3 298.9 %all-gather.11.cloned.1.call-start = ((), (), s32[]{:S(2)}) async-start(), calls=%async_computation.6 | async-start | bytes 5242880 | tf_op jit(solution)/shard_map/all_gather | solution.py:56
Sparse Core Ops, SparseCore 0:
  39.0 144.7 reduce-scatter.1
  194.9 81.0 all-gather.4
  278.2 53.7 all-gather.6
  372.4 200.7 all-gather.8
  590.4 80.7 all-gather.10
where the time goes:
time: 695 us; the launch traced here: 694 us
  waiting for transfers between devices  573 us (82%)
  matrix products  68.7 us (10%)
  blocking collectives  19.2 us (3%)
  between operations  13.8 us (2%)
  other arithmetic  9.16 us (1%)
    all_gather x1, waiting for transfers between devices, shards(): lax.all_gather(off_diag, 'dp', axis=0, tiled=True)  198 us
    reduce_scatter x1, waiting for transfers between devices, shards(): lax.psum_scatter(partial_value, 'feat', scatter_dimension=1, tiled=True)  145 us
    all_gather x1, waiting for transfers between devices, shards(): lax.all_gather(grad_proj, 'feat', axis=1, tiled=True)  80.9 us
    all_gather x1, waiting for transfers between devices, whole_rows(): return lax.all_gather(centered, 'feat', axis=1, tiled=True)  80.5 us
    all_gather x1, waiting for transfers between devices, shards(): piece = lax.all_gather(centered, 'dp', axis=0, tiled=True)  46.1 us
    all_to_all x1, waiting for transfers between devices, shards(): lax.all_to_all(cent_full, 'dp', split_axis=1, concat_axis=0, tiled=True)  22.7 us
    dot_general x1, matrix products, shards(): lax.dot_general(cent_x, piece, (((0,), (0,)), ((), ())), preferred_elemen...  17.6 us
    dot_general x1, matrix products, shards(): jnp.dot(activated, weight, preferred_element_type=jnp.float32)  17.4 us
  transfers between devices with their start and end apart: 6, of which 6 were waited for; matrix products, arithmetic and copies ran while one was open for 1% of the time, Pallas kernels for 0%

commit v1 on v0

v1 whole, which is shorter than its diff:
```python
import jax
import jax.numpy as jnp
from jax import lax
from jax.sharding import PartitionSpec as P


def shards(features, bn_gain, bn_shift, weight):
    dp_count = lax.axis_size("dp")
    feat_count = lax.axis_size("feat")
    local_rows = features.shape[0]
    images = local_rows * dp_count
    hidden = features.astype(jnp.float32)
    col_sums, col_squares = lax.psum((jnp.sum(hidden, 0), jnp.sum(hidden * hidden, 0)), "dp")
    mean_h = col_sums / images
    var_h = col_squares / images - mean_h * mean_h
    normed = (hidden - mean_h) * lax.rsqrt(var_h + 1e-05) * bn_gain + bn_shift
    activated = jnp.maximum(normed, 0.0).astype(jnp.bfloat16)
    partial_value = jnp.dot(activated, weight, preferred_element_type=jnp.float32).astype(jnp.bfloat16)
    proj_f = lax.psum_scatter(partial_value, "feat", scatter_dimension=1, tiled=True).astype(jnp.float32)
    proj_mean = lax.psum(jnp.sum(proj_f, 0), "dp") / images
    centered = (proj_f - proj_mean).astype(jnp.bfloat16)
    cent_full = lax.all_gather(centered, "feat", axis=1, tiled=True)
    piece = lax.all_gather(centered, "dp", axis=0, tiled=True)
    cent_x = lax.all_to_all(cent_full, "dp", split_axis=1, concat_axis=0, tiled=True)

    gram = lax.psum(
        lax.dot_general(centered, piece, (((1,), (1,)), ((), ())), preferred_element_type=jnp.float32),
        "feat",
    )
    piece_f = piece.astype(jnp.float32)
    proj_var = jnp.sum(piece_f * piece_f, 0) / (images - 1)
    spread = jnp.sqrt(proj_var + 0.0001)
    scale_up = images / (images - 1)
    active = jnp.where(spread < 1.0, 1.0 / spread, 0.0)
    factor = lax.all_gather(
        4.0 * scale_up * proj_var + 25.0 * scale_up * active, "feat", axis=0, tiled=True
    )
    scaled = (cent_full.astype(jnp.float32) * factor).astype(jnp.bfloat16)
    dims = (((1,), (1,)), ((), ()))
    through = lax.dot_general(cent_full, weight, dims, preferred_element_type=jnp.float32)
    direct = lax.dot_general(scaled, weight, dims, preferred_element_type=jnp.float32)
    through_all = lax.all_gather(through.astype(jnp.bfloat16), "dp", axis=0, tiled=True)

    covariance = lax.dot_general(
        cent_x, piece, (((0,), (0,)), ((), ())), preferred_element_type=jnp.float32
    ) / (images - 1)

    own = lax.axis_index("dp") * local_rows + jnp.arange(local_rows, dtype=jnp.int32)[:, None]
    same = own == jnp.arange(images, dtype=jnp.int32)[None, :]
    gram = gram * (4.0 * scale_up / (images - 1))
    diag = jnp.sum(jnp.where(same, gram, 0.0), 1, keepdims=True)
    rest = jnp.where(same, 0.0, gram).astype(jnp.bfloat16)
    grad_in = (
        jnp.dot(rest, through_all, preferred_element_type=jnp.float32) + diag * through - direct
    )
    return (covariance, grad_in.astype(jnp.bfloat16))


def solution(mesh):
    in_specs = (P(("groups", "dp"), "feat"), P("feat"), P("feat"), P("feat", None))
    out_specs = (P(("groups", "dp"), "feat"), P(("groups", "dp"), "feat"))
    return jax.shard_map(shards, mesh=mesh, in_specs=in_specs, out_specs=out_specs, check_vma=False)
```

time: 695 us -> 373 us (0.54)
  waiting for transfers between devices: 573 us -> 230 us
  blocking collectives: 19.2 us -> 33.1 us
  matrix products: 68.7 us -> 76.1 us
    all_gather x3 -> x2, waiting for transfers between devices: 359 us -> 78.1 us  [the longest x1 78.1 us: shards(): cent_full = lax.all_gather(centered, 'feat', axis=1, tiled=True)]
    reduce_scatter x1, waiting for transfers between devices: 145 us -> 77.2 us  [shards(): lax.psum_scatter(partial_value, 'feat', scatter_dimension=1, tiled=True)]
    all_gather x0 -> x1, blocking collectives: none -> 13.5 us  [shards(): lax.all_gather(4.0 * scale_up * proj_var + 25.0 * scale_up * active, 'fea...]
    all_gather x1, waiting for transfers between devices: 46.1 us -> 33.4 us  [shards(): piece = lax.all_gather(centered, 'dp', axis=0, tiled=True)]
    dot_general x2 -> x4, matrix products: 33.7 us -> 43.8 us  [the longest x1 17.4 us: shards(): lax.dot_general(scaled, weight, dims, preferred_element_type=jnp.float32)]
    psum x0 -> x1, waiting for transfers between devices: none -> 9.88 us  [shards(): lax.psum(lax.dot_general(centered, piece, (((1,), (1,)), ((), ())), prefe...]
    all_to_all x1, waiting for transfers between devices: 22.7 us -> 30.3 us  [shards(): lax.all_to_all(cent_full, 'dp', split_axis=1, concat_axis=0, tiled=True)]
  transfers between devices with their start and end apart: 6 -> 6, of which waited for: 6 -> 5; matrix products, arithmetic and copies ran while one was open for 1% -> 12% of each run, Pallas kernels for 0% -> 0%
where the time goes in v1:
time: 373 us
  waiting for transfers between devices  230 us (62%)
  matrix products  76.1 us (20%)
  blocking collectives  33.1 us (9%)
  between operations  13.8 us (4%)
  other arithmetic  9.99 us (3%)
  starting transfers between devices  5.14 us (1%)
  local copies, waits for them, and re-layouts  4.82 us (1%)
    all_gather x1, waiting for transfers between devices, shards(): cent_full = lax.all_gather(centered, 'feat', axis=1, tiled=True)  78.1 us
    reduce_scatter x1, waiting for transfers between devices, shards(): lax.psum_scatter(partial_value, 'feat', scatter_dimension=1, tiled=True)  77.2 us
    all_gather x1, waiting for transfers between devices, shards(): piece = lax.all_gather(centered, 'dp', axis=0, tiled=True)  33.4 us
    all_to_all x1, waiting for transfers between devices, shards(): lax.all_to_all(cent_full, 'dp', split_axis=1, concat_axis=0, tiled=True)  30.3 us
    dot_general x1, matrix products, shards(): lax.dot_general(scaled, weight, dims, preferred_element_type=jnp.float32)  17.4 us
    dot_general x1, matrix products, shards(): lax.dot_general(cent_full, weight, dims, preferred_element_type=jnp.float32)  16.7 us
    dot_general x1, matrix products, shards(): jnp.dot(activated, weight, preferred_element_type=jnp.float32)  16.7 us
    dot_general x1, matrix products, shards(): lax.dot_general(cent_x, piece, (((0,), (0,)), ((), ())), preferred_elemen...  15.5 us
  transfers between devices with their start and end apart: 6, of which 5 were waited for; matrix products, arithmetic and copies ran while one was open for 12% of the time, Pallas kernels for 0%

profile of v1, /device:TPU:0, one launch (start us, length us, event | category | flops | bytes accessed | tf_op | source)
XLA Modules:
  0.0 372.7 jit_solution(6901499173663036275)
XLA Ops:
  7.2 0.0 reduce-scatter.2.cloned.1.call-start
  7.2 1.5 convert_reduce_fusion
  8.7 12.7 %all-reduce = (f32[2048]{0:T(1024)S(1)}, f32[2048]{0:T(1024)S(1)}) all-reduce(f32[2048]{0:T(1024)S(1)} %get-tuple-element.3, f32[2048]{0:T(1024)S(1)} %get-tuple-element.2), channel_id=1, replica_groups=mesh['groups'=2,'feat'=4,'dp'=4] {'dp'}, use_global_device_ids=true, to_apply=%region_3.0 | all-reduce | flops 4096 | bytes 32768 | tf_op jit(solution)/shard_map/psum | solution.py:13
  21.4 16.7 %convolution_convert_fusion = bf16[256,8192]{1,0:T(8,128)(2,1)} fusion(bf16[2048,8192]{1,0:T(8,128)(2,1)} %param.7, bf16[256,2048]{1,0:T(8,128)(2,1)} %param.4, f32[2048]{0:T(1024)} %param.6, f32[2048]{0:T(1024)} %param.5, f32[2048]{0:T(1024)S(1)} %get-tuple-element.7, f32[2048]{0:T(1024)S(1)} %get-tuple-element.6), kind=kOutput, calls=%fused_computation | convolution fusion | flops 8595701760 | bytes 38830080 | tf_op jit(solution)/shard_map/dot_general | solution.py:18
  38.1 0.0 reduce-scatter.2.cloned.1.call-update
  38.2 0.0 all-gather.6.cloned.1.call-start
  38.2 77.2 %reduce-scatter.2.cloned.1.call-done = bf16[256,2048]{1,0:T(8,128)(2,1)} async-done(((bf16[256,8192]{1,0:T(8,128)(2,1)}), bf16[256,2048]{1,0:T(8,128)(2,1)}) %reduce-scatter.2.cloned.1.call-update) | async-done | bytes 1048592 | tf_op jit(solution)/shard_map/reduce_scatter | solution.py:19
  115.4 1.4 convert_reduce_fusion.1
  116.8 7.0 %psum.30 = f32[2048]{0:T(1024)S(1)} all-reduce(f32[2048]{0:T(1024)S(1)} %convert_reduce_fusion.1), channel_id=1, replica_groups=mesh['groups'=2,'feat'=4,'dp'=4] {'dp'}, use_global_device_ids=true, to_apply=%region_6.0 | all-reduce | flops 2048 | bytes 16384 | tf_op jit(solution)/shard_map/psum | solution.py:20
  123.8 2.4 fusion.4
  126.3 0.0 all-gather.6.cloned.1.call-update
  126.3 0.0 all-gather.4.cloned.1.call-start
  126.3 0.7 all-gather.4.cloned.1.call-update
  127.0 0.0 all-reduce.3.cloned.1.call-start
  127.1 33.4 %all-gather.6.cloned.1.call-done = bf16[1024,2048]{1,0:T(8,128)(2,1)} async-done(((bf16[256,2048]{1,0:T(8,128)(2,1)}), bf16[1024,2048]{1,0:T(8,128)(2,1)}) %all-gather.6.cloned.1.call-update) | async-done | bytes 4194320 | tf_op jit(solution)/shard_map/all_gather | solution.py:23
  160.5 4.8 %fusion.24 = f32[256,1024]{1,0:T(8,128)} fusion(bf16[256,2048]{1,0:T(8,128)(2,1)} %fusion.4, bf16[1024,2048]{1,0:T(8,128)(2,1)} %all-gather.6.cloned.1.call-done), kind=kOutput, calls=%fused_computation.43 | convolution fusion | flops 1073741824 | bytes 6291456 | tf_op jit(solution)/shard_map/dot_general | solution.py:27
  165.3 0.0 all-reduce.3.cloned.1.call-update
  165.3 0.0 all-gather.8.cloned.1.call-start
  165.4 78.1 %all-gather.4.cloned.1.call-done = bf16[256,8192]{1,0:T(8,128)(2,1)} async-done(((bf16[256,2048]{1,0:T(8,128)(2,1)}), bf16[256,8192]{1,0:T(8,128)(2,1)}) %all-gather.4.cloned.1.call-update) | async-done | bytes 4194320 | tf_op jit(solution)/shard_map/all_gather | solution.py:22
  243.5 16.7 %fusion.23 = (bf16[256,2048]{1,0:T(8,128)(2,1)}, f32[256,2048]{1,0:T(8,128)S(1)}) fusion(bf16[256,8192]{1,0:T(8,128)(2,1)} %all-gather.4.cloned.1.call-done, bf16[2048,8192]{1,0:T(8,128)(2,1)} %param.7), kind=kOutput, calls=%fused_computation.42 | convolution fusion | flops 8590458880 | bytes 40894464 | tf_op jit(solution)/shard_map/dot_general | solution.py:40
  260.2 0.0 all-gather.8.cloned.1.call-update
  260.3 4.8 %copy.10 = bf16[32,4,8,2048]{3,2,0,1:T(8,128)(2,1)} copy(bf16[32,4,8,2048]{3,2,1,0:T(8,128)(2,1)} %bitcast.17) | data formatting | bytes 8388608 | tf_op jit(solution)/shard_map/all_to_all | solution.py:24
  265.1 4.9 %all-to-all-start = ((bf16[256,4,2048]{2,0,1:T(8,128)(2,1)}), bf16[256,4,2048]{2,0,1:T(8,128)(2,1)}, u32[]{:S(2)}, u32[]{:S(2)}) async-start(bf16[256,4,2048]{2,0,1:T(8,128)(2,1)} %bitcast.16), calls=%async_computation.1 | async-start | bytes 8388608 | tf_op jit(solution)/shard_map/all_to_all | solution.py:24
  270.0 3.1 multiply_reduce_fusion
  273.1 13.5 %all_gather.15 = f32[8192]{0:T(1024)S(1)} all-gather(f32[2048]{0:T(1024)S(1)} %multiply_add_fusion), channel_id=1, replica_groups=mesh['groups'=2,'feat'=4,'dp'=4] {'feat'}, dimensions={0}, use_global_device_ids=true | all-gather | bytes 40960 | tf_op jit(solution)/shard_map/all_gather | solution.py:35
  286.6 9.9 %all-reduce.3.cloned.1.call-done = f32[256,1024]{1,0:T(8,128)} async-done(((f32[256,1024]{1,0:T(8,128)}), f32[256,1024]{1,0:T(8,128)}) %all-reduce.3.cloned.1.call-update) | async-done | bytes 1048592 | tf_op jit(solution)/shard_map/psum | solution.py:26
  296.5 1.5 select_reduce_fusion
  298.0 30.3 %all-to-all-done = bf16[256,4,2048]{2,0,1:T(8,128)(2,1)} async-done(((bf16[256,4,2048]{2,0,1:T(8,128)(2,1)}), bf16[256,4,2048]{2,0,1:T(8,128)(2,1)}, u32[]{:S(2)}, u32[]{:S(2)}) %all-to-all-start) | async-done | bytes 4194336 | tf_op jit(solution)/shard_map/all_to_all | solution.py:24
  328.3 0.0 copy-start
  328.3 15.5 %convolution_multiply_fusion = f32[2048,2048]{1,0:T(8,128)} fusion(bf16[1024,2048]{1,0:T(8,128)(2,1)} %bitcast.1, bf16[1024,2048]{1,0:T(8,128)(2,1)} %all-gather.6.cloned.1.call-done), kind=kOutput, calls=%fused_computation.1 | convolution fusion | flops 8594128896 | bytes 25165824 | tf_op jit(solution)/shard_map/dot_general | solution.py:44
  343.9 0.0 all-gather.8.cloned.1.call-done
  343.9 0.0 copy-done
  343.9 4.9 %convolution_add_fusion = f32[256,2048]{1,0:T(8,128)} fusion(bf16[1024,2048]{1,0:T(8,128)(2,1)} %all-gather.8.cloned.1.call-done, f32[256,2048]{1,0:T(8,128)S(1)} %get-tuple-element.9, f32[256]{0:T(256)S(1)} %select_reduce_fusion, f32[256,1024]{1,0:T(8,128)S(1)} %copy-done, s32[256]{0:T(256)S(1)} %iota_add_fusion), kind=kOutput, calls=%fused_computation.12 | convolution fusion | flops 1075838976 | bytes 9439232 | tf_op jit(solution)/shard_map/dot_general | solution.py:54
  348.8 17.4 %fusion.3 = bf16[256,2048]{1,0:T(8,128)(2,1)} fusion(f32[256,2048]{1,0:T(8,128)} %convolution_add_fusion, bf16[2048,8192]{1,0:T(8,128)(2,1)} %param.7, bf16[256,8192]{1,0:T(8,128)(2,1)} %all-gather.4.cloned.1.call-done, f32[8192]{0:T(1024)S(1)} %all_gather.15), kind=kOutput, calls=%fused_computation.14 | convolution fusion | flops 8597274624 | bytes 40927232 | tf_op jit(solution)/shard_map/dot_general | solution.py:41
  (4 shorter events, 0.0 us)
Async XLA Ops:
  7.2 108.3 %reduce-scatter.2.cloned.1.call-start = ((), (), s32[]{:S(2)}) async-start(), calls=%async_computation.2 | async-start | bytes 5242880 | tf_op jit(solution)/shard_map/reduce_scatter | solution.py:19
  38.2 122.3 %all-gather.6.cloned.1.call-start = ((), (), s32[]{:S(2)}) async-start(), calls=%async_computation.4 | async-start | bytes 5242880 | tf_op jit(solution)/shard_map/all_gather | solution.py:23
  126.3 117.2 %all-gather.4.cloned.1.call-start = ((), (), s32[]{:S(2)}) async-start(), calls=%async_computation.3 | async-start | bytes 5242880 | tf_op jit(solution)/shard_map/all_gather | solution.py:22
  127.0 169.5 %all-reduce.3.cloned.1.call-start = ((), (), s32[]{:S(2)}) async-start(), calls=%async_computation.5 | async-start | bytes 2097152 | tf_op jit(solution)/shard_map/psum | solution.py:26
  165.3 178.5 %all-gather.8.cloned.1.call-start = ((), (), s32[]{:S(2)}) async-start(), calls=%async_computation.6 | async-start | bytes 5242880 | tf_op jit(solution)/shard_map/all_gather | solution.py:42
  265.1 63.3 %all-to-all-start = ((bf16[256,4,2048]{2,0,1:T(8,128)(2,1)}), bf16[256,4,2048]{2,0,1:T(8,128)(2,1)}, u32[]{:S(2)}, u32[]{:S(2)}) async-start(bf16[256,4,2048]{2,0,1:T(8,128)(2,1)} %bitcast.16), calls=%async_computation.1 | async-start | bytes 8388608 | tf_op jit(solution)/shard_map/all_to_all | solution.py:24
  328.3 15.5 %copy-start = (f32[256,1024]{1,0:T(8,128)S(1)}, f32[256,1024]{1,0:T(8,128)}, u32[]{:S(2)}) copy-start(f32[256,1024]{1,0:T(8,128)} %all-reduce.3.cloned.1.call-done) | copy-start | bytes 3145732
Sparse Core Ops, SparseCore 0:
  38.3 77.0 reduce-scatter.1
  126.4 34.0 all-gather.5
  162.7 80.7 all-gather.3
  245.9 50.6 all-reduce.2
  298.5 43.7 all-gather.7

commit v2 on v1

--- a/solution.py
+++ b/solution.py
@@ -2,6 +2,42 @@
 import jax.numpy as jnp
 from jax import lax
 from jax.sharding import PartitionSpec as P
+
+
+def swap(value, distance):
+    count = lax.axis_size("dp")
+    return lax.ppermute(value, "dp", [(i, i ^ distance) for i in range(count)])
+
+
+def block_order(count):
+    order = [0]
+    bit = count // 2
+    while bit:
+        order = order + [o ^ bit for o in order]
+        bit //= 2
+    return order
+
+
+def gather_rows(value):
+    bit = lax.axis_size("dp") // 2
+    while bit:
+        value = jnp.concatenate([value, swap(value, bit)], 0)
+        bit //= 2
+    return value
+
+
+def column_blocks(full):
+    count = lax.axis_size("dp")
+    width = full.shape[1] // count
+    me = lax.axis_index("dp")
+    return [
+        lax.dynamic_slice_in_dim(full, (me ^ o) * width, width, 1) for o in block_order(count)
+    ]
+
+
+def exchange(blocks):
+    order = block_order(lax.axis_size("dp"))
+    return jnp.concatenate([swap(b, o) if o else b for b, o in zip(blocks, order)], 0)
 
 
 def shards(features, bn_gain, bn_shift, weight):
@@ -20,12 +56,10 @@
     proj_mean = lax.psum(jnp.sum(proj_f, 0), "dp") / images
     centered = (proj_f - proj_mean).astype(jnp.bfloat16)
     cent_full = lax.all_gather(centered, "feat", axis=1, tiled=True)
-    piece = lax.all_gather(centered, "dp", axis=0, tiled=True)
-    cent_x = lax.all_to_all(cent_full, "dp", split_axis=1, concat_axis=0, tiled=True)
+    piece = gather_rows(centered)
 
-    gram = lax.psum(
-        lax.dot_general(centered, piece, (((1,), (1,)), ((), ())), preferred_element_type=jnp.float32),
-        "feat",
+    gram = lax.dot_general(
+        centered, piece, (((1,), (1,)), ((), ())), preferred_element_type=jnp.float32
     )
     piece_f = piece.astype(jnp.float32)
     proj_var = jnp.sum(piece_f * piece_f, 0) / (images - 1)
@@ -35,17 +69,22 @@
     factor = lax.all_gather(
         4.0 * scale_up * proj_var + 25.0 * scale_up * active, "feat", axis=0, tiled=True
     )
+    cent_full, factor, _ = lax.optimization_barrier((cent_full, factor, gram))
+    gram = lax.psum(gram, "feat")
+    cent_full, cuts = lax.optimization_barrier((cent_full, column_blocks(cent_full)))
+    cent_x = exchange(cuts)
     scaled = (cent_full.astype(jnp.float32) * factor).astype(jnp.bfloat16)
     dims = (((1,), (1,)), ((), ()))
     through = lax.dot_general(cent_full, weight, dims, preferred_element_type=jnp.float32)
     direct = lax.dot_general(scaled, weight, dims, preferred_element_type=jnp.float32)
-    through_all = lax.all_gather(through.astype(jnp.bfloat16), "dp", axis=0, tiled=True)
+    through_all = gather_rows(through.astype(jnp.bfloat16))
 
     covariance = lax.dot_general(
         cent_x, piece, (((0,), (0,)), ((), ())), preferred_element_type=jnp.float32
     ) / (images - 1)
 
-    own = lax.axis_index("dp") * local_rows + jnp.arange(local_rows, dtype=jnp.int32)[:, None]
+    gram, covariance = lax.optimization_barrier((gram, covariance))
+    own = jnp.arange(local_rows, dtype=jnp.int32)[:, None]
     same = own == jnp.arange(images, dtype=jnp.int32)[None, :]
     gram = gram * (4.0 * scale_up / (images - 1))
     diag = jnp.sum(jnp.where(same, gram, 0.0), 1, keepdims=True)

time: 373 us -> 328 us (0.88)
  waiting for transfers between devices: 230 us -> 179 us
  other arithmetic: 9.99 us -> 14.9 us
    ppermute x0 -> x7, waiting for transfers between devices: none -> 73.9 us  [swap(): return lax.ppermute(value, 'dp', [(i, i ^ distance) for i in range(count)])]
    all_gather x1, waiting for transfers between devices: 78.1 us -> 28 us  [shards(): cent_full = lax.all_gather(centered, 'feat', axis=1, tiled=True)]
    all_gather x2 -> x0, waiting for transfers between devices: 33.4 us -> none  [the longest x1 33.4 us: shards(): piece = lax.all_gather(centered, 'dp', axis=0, tiled=True)]
    all_to_all x1 -> x0, waiting for transfers between devices: 30.3 us -> none  [shards(): lax.all_to_all(cent_full, 'dp', split_axis=1, concat_axis=0, tiled=True)]
    psum x1, waiting for transfers between devices: 9.88 us -> 0.01 us  [shards(): gram = lax.psum(gram, 'feat')]
    concatenate x0 -> x2, other arithmetic: none -> 5.94 us  [gather_rows(): value = jnp.concatenate([value, swap(value, bit)], 0)]
    all_to_all x1 -> x0, starting transfers between devices: 4.94 us -> none  [shards(): lax.all_to_all(cent_full, 'dp', split_axis=1, concat_axis=0, tiled=True)]
    all_to_all x1 -> x0, local copies, waits for them, and re-layouts: 4.81 us -> none  [shards(): lax.all_to_all(cent_full, 'dp', split_axis=1, concat_axis=0, tiled=True)]
  transfers between devices with their start and end apart: 6 -> 10, of which waited for: 5 -> 7; matrix products, arithmetic and copies ran while one was open for 12% -> 14% of each run, Pallas kernels for 0% -> 0%
where the time goes in v2:
time: 328 us; the launch traced here: 327 us
  waiting for transfers between devices  179 us (55%)
  matrix products  76.1 us (23%)
  blocking collectives  35.1 us (11%)
  other arithmetic  14.9 us (5%)
  between operations  13.8 us (4%)
  starting transfers between devices  4.41 us (1%)
  local copies, waits for them, and re-layouts  3.97 us (1%)
    reduce_scatter x1, waiting for transfers between devices, shards(): lax.psum_scatter(partial_value, 'feat', scatter_dimension=1, tiled=True)  77.2 us
    ppermute x7, waiting for transfers between devices, swap(): return lax.ppermute(value, 'dp', [(i, i ^ distance) for i in range(count)])  73.9 us
    all_gather x1, waiting for transfers between devices, shards(): cent_full = lax.all_gather(centered, 'feat', axis=1, tiled=True)  28 us
    dot_general x1, matrix products, shards(): lax.dot_general(cent_full, weight, dims, preferred_element_type=jnp.float32)  17.4 us
    dot_general x1, matrix products, shards(): lax.dot_general(scaled, weight, dims, preferred_element_type=jnp.float32)  17.3 us
    dot_general x1, matrix products, shards(): jnp.dot(activated, weight, preferred_element_type=jnp.float32)  16.7 us
    all_gather x1, blocking collectives, shards(): lax.all_gather(4.0 * scale_up * proj_var + 25.0 * scale_up * active, 'fea...  15.5 us
    dot_general x1, matrix products, shards(): lax.dot_general(cent_x, piece, (((0,), (0,)), ((), ())), preferred_elemen...  14.7 us
  transfers between devices with their start and end apart: 10, of which 7 were waited for; matrix products, arithmetic and copies ran while one was open for 14% of the time, Pallas kernels for 0%

profile of v2, /device:TPU:0, one launch (start us, length us, event | category | flops | bytes accessed | tf_op | source)
XLA Modules:
  0.0 327.4 jit_solution(5208170377373880028)
XLA Ops:
  7.2 0.0 reduce-scatter.2.cloned.1.call-start
  7.2 1.5 convert_reduce_fusion
  8.7 12.7 %all-reduce = (f32[2048]{0:T(1024)S(1)}, f32[2048]{0:T(1024)S(1)}) all-reduce(f32[2048]{0:T(1024)S(1)} %get-tuple-element.21, f32[2048]{0:T(1024)S(1)} %get-tuple-element.20), channel_id=1, replica_groups=mesh['groups'=2,'feat'=4,'dp'=4] {'dp'}, use_global_device_ids=true, to_apply=%region_3.0 | all-reduce | flops 4096 | bytes 32768 | tf_op jit(solution)/shard_map/psum | solution.py:49
  21.4 16.7 %convolution_convert_fusion = bf16[256,8192]{1,0:T(8,128)(2,1)} fusion(bf16[2048,8192]{1,0:T(8,128)(2,1)} %param.7, bf16[256,2048]{1,0:T(8,128)(2,1)} %param.4, f32[2048]{0:T(1024)} %param.6, f32[2048]{0:T(1024)} %param.5, f32[2048]{0:T(1024)S(1)} %get-tuple-element.29, f32[2048]{0:T(1024)S(1)} %get-tuple-element.28), kind=kOutput, calls=%fused_computation | convolution fusion | flops 8595701760 | bytes 38830080 | tf_op jit(solution)/shard_map/dot_general | solution.py:54
  38.1 0.0 reduce-scatter.2.cloned.1.call-update
  38.2 0.0 all-gather.2.cloned.1.call-start
  38.2 77.2 %reduce-scatter.2.cloned.1.call-done = bf16[256,2048]{1,0:T(8,128)(2,1)} async-done(((bf16[256,8192]{1,0:T(8,128)(2,1)}), bf16[256,2048]{1,0:T(8,128)(2,1)}) %reduce-scatter.2.cloned.1.call-update) | async-done | bytes 1048592 | tf_op jit(solution)/shard_map/reduce_scatter | solution.py:55
  115.4 1.4 convert_reduce_fusion.1
  116.8 7.0 %psum.30 = f32[2048]{0:T(1024)S(1)} all-reduce(f32[2048]{0:T(1024)S(1)} %convert_reduce_fusion.1), channel_id=1, replica_groups=mesh['groups'=2,'feat'=4,'dp'=4] {'dp'}, use_global_device_ids=true, to_apply=%region_6.0 | all-reduce | flops 2048 | bytes 16384 | tf_op jit(solution)/shard_map/psum | solution.py:56
  123.8 2.4 fusion.24
  126.3 0.0 copy-start
  126.3 0.0 all-gather.2.cloned.1.call-update
  126.3 0.0 all-reduce.3.cloned.1.call-start
  126.3 0.6 collective-permute-start
  126.9 23.4 %collective-permute-done = bf16[256,2048]{1,0:T(8,128)(2,1)S(1)} collective-permute-done((bf16[256,2048]{1,0:T(8,128)(2,1)}, bf16[256,2048]{1,0:T(8,128)(2,1)S(1)}, u32[]{:S(2)}, u32[]{:S(2)}) %collective-permute-start) | collective-permute-done | bytes 1048608 | tf_op jit(solution)/shard_map/ppermute | solution.py:9
  150.3 2.8 pad_maximum_fusion.1
  153.1 0.0 collective-permute-start.1
  153.1 4.5 %collective-permute-done.1 = bf16[512,2048]{1,0:T(8,128)(2,1)} collective-permute-done((bf16[512,2048]{1,0:T(8,128)(2,1)}, bf16[512,2048]{1,0:T(8,128)(2,1)}, u32[]{:S(2)}, u32[]{:S(2)}) %collective-permute-start.1) | collective-permute-done | bytes 2097184 | tf_op jit(solution)/shard_map/ppermute | solution.py:9
  157.6 0.0 copy-done
  157.6 2.2 multiply_reduce_fusion
  159.8 15.5 %all_gather.7 = f32[8192]{0:T(1024)S(1)} all-gather(f32[2048]{0:T(1024)S(1)} %multiply_add_fusion), channel_id=1, replica_groups=mesh['groups'=2,'feat'=4,'dp'=4] {'feat'}, dimensions={0}, use_global_device_ids=true | all-gather | bytes 40960 | tf_op jit(solution)/shard_map/all_gather | solution.py:69
  175.3 3.9 %fusion.44 = f32[256,1024]{1,0:T(8,128)} fusion(bf16[256,2048]{1,0:T(8,128)(2,1)S(1)} %copy-done, bf16[512,2048]{1,0:T(8,128)(2,1)} %collective-permute-done.1, bf16[256,2048]{1,0:T(8,128)(2,1)S(1)} %collective-permute-done), kind=kOutput, calls=%fused_computation.61 | convolution fusion | flops 1086324736 | bytes 5242880 | tf_op jit(solution)/shard_map/dot_general | solution.py:61
  179.2 28.0 %all-gather.2.cloned.1.call-done = bf16[256,8192]{1,0:T(8,128)(2,1)} async-done(((bf16[256,2048]{1,0:T(8,128)(2,1)}), bf16[256,8192]{1,0:T(8,128)(2,1)}) %all-gather.2.cloned.1.call-update) | async-done | bytes 4194320 | tf_op jit(solution)/shard_map/all_gather | solution.py:58
  207.2 4.0 %constant_dynamic-slice_fusion = (bf16[256,2048]{1,0:T(8,128)(2,1)}, bf16[256,2048]{1,0:T(8,128)(2,1)}, bf16[256,2048]{1,0:T(8,128)(2,1)}, bf16[256,2048]{1,0:T(8,128)(2,1)S(1)}) fusion(bf16[256,8192]{1,0:T(8,128)(2,1)} %all-gather.2.cloned.1.call-done, s32[]{:T(128)S(6)} %select_n.28, s32[]{:T(128)S(6)} %select_n.27, s32[]{:T(128)S(6)} %select_n.26, ...), kind=kLoop, calls=%fused_computation.52 | loop fusion | bytes 8388624 | tf_op jit(solution)/shard_map/dynamic_slice | solution.py:34
  211.2 17.4 %fusion.45 = (bf16[256,2048]{1,0:T(8,128)(2,1)}, f32[256,2048]{1,0:T(8,128)}) fusion(bf16[256,8192]{1,0:T(8,128)(2,1)} %all-gather.2.cloned.1.call-done, bf16[2048,8192]{1,0:T(8,128)(2,1)} %param.7), kind=kOutput, calls=%fused_computation.62 | convolution fusion | flops 8590458880 | bytes 40894464 | tf_op jit(solution)/shard_map/dot_general | solution.py:78
  228.6 1.5 collective-permute-start.5
  230.0 0.0 all-reduce.3.cloned.1.call-update
  230.1 0.1 collective-permute-start.4
  230.1 0.7 collective-permute-start.3
  230.8 1.5 collective-permute-start.2
  232.3 22.7 %collective-permute-done.5 = bf16[256,2048]{1,0:T(8,128)(2,1)} collective-permute-done((bf16[256,2048]{1,0:T(8,128)(2,1)}, bf16[256,2048]{1,0:T(8,128)(2,1)}, u32[]{:S(2)}, u32[]{:S(2)}) %collective-permute-start.5) | collective-permute-done | bytes 1048608 | tf_op jit(solution)/shard_map/ppermute | solution.py:9
  254.9 3.2 pad_maximum_fusion.2
  258.1 0.0 collective-permute-start.6
  258.1 17.3 %fusion = f32[256,2048]{1,0:T(8,128)} fusion(bf16[2048,8192]{1,0:T(8,128)(2,1)} %param.7, bf16[256,8192]{1,0:T(8,128)(2,1)} %all-gather.2.cloned.1.call-done, f32[8192]{0:T(1024)S(1)} %all_gather.7), kind=kOutput, calls=%fused_computation.4 | convolution fusion | flops 8596226048 | bytes 39878656 | tf_op jit(solution)/shard_map/dot_general | solution.py:79
  275.4 1.0 collective-permute-done.4
  276.4 0.0 collective-permute-done.3
  276.4 22.3 %collective-permute-done.2 = bf16[256,2048]{1,0:T(8,128)(2,1)} collective-permute-done((bf16[256,2048]{1,0:T(8,128)(2,1)}, bf16[256,2048]{1,0:T(8,128)(2,1)}, u32[]{:S(2)}, u32[]{:S(2)}) %collective-permute-start.2) | collective-permute-done | bytes 1048608 | tf_op jit(solution)/shard_map/ppermute | solution.py:9
  298.7 14.7 %convolution_multiply_fusion = f32[2048,2048]{1,0:T(8,128)} fusion(bf16[256,2048]{1,0:T(8,128)(2,1)} %collective-permute-done.4, bf16[256,2048]{1,0:T(8,128)(2,1)} %collective-permute-done.3, bf16[256,2048]{1,0:T(8,128)(2,1)} %collective-permute-done.2, bf16[256,2048]{1,0:T(8,128)(2,1)S(1)} %get-tuple-element.12, ...), kind=kOutput, calls=%fused_computation.1 | convolution fusion | flops 8623489024 | bytes 25165824 | tf_op jit(solution)/shard_map/dot_general | solution.py:82
  313.4 0.0 all-reduce.3.cloned.1.call-done
  313.4 1.3 select_reduce_fusion
  314.7 0.0 collective-permute-done.6
  314.8 6.1 %fusion.21 = bf16[256,2048]{1,0:T(8,128)(2,1)} fusion(f32[256,2048]{1,0:T(8,128)} %fusion, bf16[512,2048]{1,0:T(8,128)(2,1)} %collective-permute-done.6, bf16[256,2048]{1,0:T(8,128)(2,1)} %collective-permute-done.5, bf16[256,2048]{1,0:T(8,128)(2,1)} %get-tuple-element.30, f32[256,2048]{1,0:T(8,128)} %get-tuple-element.31, f32[256]{0:T(256)S(1)} %select_reduce_fusion, ...), kind=kOutput, calls=%fused_computation.27 | convolution fusion | flops 1089470464 | bytes 10486784 | tf_op jit(solution)/shard_map/dot_general | solution.py:93
  (3 shorter events, 0.0 us)
Async XLA Ops:
  7.2 108.3 %reduce-scatter.2.cloned.1.call-start = ((), (), s32[]{:S(2)}) async-start(), calls=%async_computation.1 | async-start | bytes 5242880 | tf_op jit(solution)/shard_map/reduce_scatter | solution.py:55
  38.2 169.0 %all-gather.2.cloned.1.call-start = ((), (), s32[]{:S(2)}) async-start(), calls=%async_computation.3 | async-start | bytes 5242880 | tf_op jit(solution)/shard_map/all_gather | solution.py:58
  126.3 31.4 %copy-start = (bf16[256,2048]{1,0:T(8,128)(2,1)S(1)}, bf16[256,2048]{1,0:T(8,128)(2,1)}, u32[]{:S(2)}) copy-start(bf16[256,2048]{1,0:T(8,128)(2,1)} %fusion.24) | copy-start | bytes 3145732
  126.3 187.1 %all-reduce.3.cloned.1.call-start = ((), (), s32[]{:S(2)}) async-start(), calls=%async_computation.2 | async-start | bytes 2097152 | tf_op jit(solution)/shard_map/psum | solution.py:73
  126.3 24.0 %collective-permute-start = (bf16[256,2048]{1,0:T(8,128)(2,1)}, bf16[256,2048]{1,0:T(8,128)(2,1)S(1)}, u32[]{:S(2)}, u32[]{:S(2)}) collective-permute-start(bf16[256,2048]{1,0:T(8,128)(2,1)} %fusion.24), channel_id=1, source_target_pairs={{0,2},{1,3},{2,0},{3,1},{4,6},{5,7},{6,4},{7,5},{8,10},{9,11},{10,... | collective-permute-start | bytes 3145736 | tf_op jit(solution)/shard_map/ppermute | solution.py:9
  153.1 4.5 %collective-permute-start.1 = (bf16[512,2048]{1,0:T(8,128)(2,1)}, bf16[512,2048]{1,0:T(8,128)(2,1)}, u32[]{:S(2)}, u32[]{:S(2)}) collective-permute-start(bf16[512,2048]{1,0:T(8,128)(2,1)} %pad_maximum_fusion.1), channel_id=1, source_target_pairs={{0,1},{1,0},{2,3},{3,2},{4,5},{5,4},{6,7},{7,6},{8,9},{9,8},{10,11... | collective-permute-start | bytes 6291464 | tf_op jit(solution)/shard_map/ppermute | solution.py:9
  228.6 26.4 %collective-permute-start.5 = (bf16[256,2048]{1,0:T(8,128)(2,1)}, bf16[256,2048]{1,0:T(8,128)(2,1)}, u32[]{:S(2)}, u32[]{:S(2)}) collective-permute-start(bf16[256,2048]{1,0:T(8,128)(2,1)} %get-tuple-element.30), channel_id=1, source_target_pairs={{0,2},{1,3},{2,0},{3,1},{4,6},{5,7},{6,4},{7,5},{8,10},{9,11},{10,... | collective-permute-start | bytes 3145736 | tf_op jit(solution)/shard_map/ppermute | solution.py:9
  230.1 46.3 %collective-permute-start.4 = (bf16[256,2048]{1,0:T(8,128)(2,1)}, bf16[256,2048]{1,0:T(8,128)(2,1)}, u32[]{:S(2)}, u32[]{:S(2)}) collective-permute-start(bf16[256,2048]{1,0:T(8,128)(2,1)} %get-tuple-element.15), channel_id=1, source_target_pairs={{0,3},{1,2},{2,1},{3,0},{4,7},{5,6},{6,5},{7,4},{8,11},{9,10},{10,... | collective-permute-start | bytes 3145736 | tf_op jit(solution)/shard_map/ppermute | solution.py:9
  230.1 46.3 %collective-permute-start.3 = (bf16[256,2048]{1,0:T(8,128)(2,1)}, bf16[256,2048]{1,0:T(8,128)(2,1)}, u32[]{:S(2)}, u32[]{:S(2)}) collective-permute-start(bf16[256,2048]{1,0:T(8,128)(2,1)} %get-tuple-element.14), channel_id=1, source_target_pairs={{0,1},{1,0},{2,3},{3,2},{4,5},{5,4},{6,7},{7,6},{8,9},{9,8},{10,11... | collective-permute-start | bytes 3145736 | tf_op jit(solution)/shard_map/ppermute | solution.py:9
  230.8 67.9 %collective-permute-start.2 = (bf16[256,2048]{1,0:T(8,128)(2,1)}, bf16[256,2048]{1,0:T(8,128)(2,1)}, u32[]{:S(2)}, u32[]{:S(2)}) collective-permute-start(bf16[256,2048]{1,0:T(8,128)(2,1)} %get-tuple-element.13), channel_id=1, source_target_pairs={{0,2},{1,3},{2,0},{3,1},{4,6},{5,7},{6,4},{7,5},{8,10},{9,11},{10,... | collective-permute-start | bytes 3145736 | tf_op jit(solution)/shard_map/ppermute | solution.py:9
  258.1 56.7 %collective-permute-start.6 = (bf16[512,2048]{1,0:T(8,128)(2,1)}, bf16[512,2048]{1,0:T(8,128)(2,1)}, u32[]{:S(2)}, u32[]{:S(2)}) collective-permute-start(bf16[512,2048]{1,0:T(8,128)(2,1)} %pad_maximum_fusion.2), channel_id=1, source_target_pairs={{0,1},{1,0},{2,3},{3,2},{4,5},{5,4},{6,7},{7,6},{8,9},{9,8},{10,11... | collective-permute-start | bytes 6291464 | tf_op jit(solution)/shard_map/ppermute | solution.py:9
Sparse Core Ops, SparseCore 0:
  38.3 77.0 reduce-scatter.1
  126.4 80.7 all-gather.1
  230.2 49.4 all-reduce.2

commit v3 on v2

--- a/solution.py
+++ b/solution.py
@@ -37,7 +37,7 @@
 
 def exchange(blocks):
     order = block_order(lax.axis_size("dp"))
-    return jnp.concatenate([swap(b, o) if o else b for b, o in zip(blocks, order)], 0)
+    return [swap(b, o) if o else b for b, o in zip(blocks, order)]
 
 
 def shards(features, bn_gain, bn_shift, weight):
@@ -55,7 +55,9 @@
     proj_f = lax.psum_scatter(partial_value, "feat", scatter_dimension=1, tiled=True).astype(jnp.float32)
     proj_mean = lax.psum(jnp.sum(proj_f, 0), "dp") / images
     centered = (proj_f - proj_mean).astype(jnp.bfloat16)
-    cent_full = lax.all_gather(centered, "feat", axis=1, tiled=True)
+    half = local_rows // 2
+    upper = lax.all_gather(centered[:half], "feat", axis=1, tiled=True)
+    lower = lax.all_gather(centered[half:], "feat", axis=1, tiled=True)
     piece = gather_rows(centered)
 
     gram = lax.dot_general(
@@ -69,13 +71,17 @@
     factor = lax.all_gather(
         4.0 * scale_up * proj_var + 25.0 * scale_up * active, "feat", axis=0, tiled=True
     )
-    cent_full, factor, _ = lax.optimization_barrier((cent_full, factor, gram))
+    upper_cuts = exchange(column_blocks(upper))
+    lower, factor, _ = lax.optimization_barrier((lower, factor, gram))
     gram = lax.psum(gram, "feat")
-    cent_full, cuts = lax.optimization_barrier((cent_full, column_blocks(cent_full)))
-    cent_x = exchange(cuts)
-    scaled = (cent_full.astype(jnp.float32) * factor).astype(jnp.bfloat16)
+    lower, cuts = lax.optimization_barrier((lower, column_blocks(lower)))
+    lower_cuts = exchange(cuts)
+    cent_x = jnp.concatenate([b for pair in zip(upper_cuts, lower_cuts) for b in pair], 0)
+    cent_full = jnp.concatenate([upper, lower], 0)
     dims = (((1,), (1,)), ((), ()))
     through = lax.dot_general(cent_full, weight, dims, preferred_element_type=jnp.float32)
+    cent_full, through = lax.optimization_barrier((cent_full, through))
+    scaled = (cent_full.astype(jnp.float32) * factor).astype(jnp.bfloat16)
     direct = lax.dot_general(scaled, weight, dims, preferred_element_type=jnp.float32)
     through_all = gather_rows(through.astype(jnp.bfloat16))
 

time: 328 us -> 330 us (level)
  local copies, waits for them, and re-layouts: 3.97 us -> 20.4 us
  waiting for transfers between devices: 179 us -> 168 us
    ppermute x7 -> x10, waiting for transfers between devices: 73.9 us -> 51.2 us  [swap(): return lax.ppermute(value, 'dp', [(i, i ^ distance) for i in range(count)])]
    unnamed x2 -> x21, local copies, waits for them, and re-layouts: 0.01 us -> 11.8 us
    all_gather x1 -> x2, waiting for transfers between devices: 28 us -> 39.7 us  [the longest x1 39.7 us: shards(): upper = lax.all_gather(centered[:half], 'feat', axis=1, tiled=True)]
  transfers between devices with their start and end apart: 10 -> 14, of which waited for: 7 -> 6; matrix products, arithmetic and copies ran while one was open for 14% -> 24% of each run, Pallas kernels for 0% -> 0%
where the time goes in v3:
time: 330 us; the launch traced here: 329 us
  waiting for transfers between devices  168 us (51%)
  matrix products  74.1 us (22%)
  blocking collectives  33.5 us (10%)
  local copies, waits for them, and re-layouts  20.4 us (6%)
  between operations  13.9 us (4%)
  other arithmetic  12.7 us (4%)
  starting transfers between devices  6.3 us (2%)
    reduce_scatter x1, waiting for transfers between devices, shards(): lax.psum_scatter(partial_value, 'feat', scatter_dimension=1, tiled=True)  77.2 us
    ppermute x10, waiting for transfers between devices, swap(): return lax.ppermute(value, 'dp', [(i, i ^ distance) for i in range(count)])  51.2 us
    all_gather x1, waiting for transfers between devices, shards(): upper = lax.all_gather(centered[:half], 'feat', axis=1, tiled=True)  39.7 us
    dot_general x1, matrix products, shards(): lax.dot_general(scaled, weight, dims, preferred_element_type=jnp.float32)  17.1 us
    dot_general x1, matrix products, shards(): lax.dot_general(cent_full, weight, dims, preferred_element_type=jnp.float32)  17 us
    dot_general x1, matrix products, shards(): jnp.dot(activated, weight, preferred_element_type=jnp.float32)  16.7 us
    dot_general x1, matrix products, shards(): lax.dot_general(cent_x, piece, (((0,), (0,)), ((), ())), preferred_elemen...  13.9 us
    all_gather x1, blocking collectives, shards(): lax.all_gather(4.0 * scale_up * proj_var + 25.0 * scale_up * active, 'fea...  13.8 us
  transfers between devices with their start and end apart: 14, of which 6 were waited for; matrix products, arithmetic and copies ran while one was open for 24% of the time, Pallas kernels for 0%

profile of v3, /device:TPU:0, one launch (start us, length us, event | category | flops | bytes accessed | tf_op | source)
XLA Modules:
  0.0 329.0 jit_solution(3517404704759358985)
XLA Ops:
  7.2 0.0 reduce-scatter.2.cloned.1.call-start
  7.2 1.5 convert_reduce_fusion
  8.7 12.7 %all-reduce = (f32[2048]{0:T(1024)S(1)}, f32[2048]{0:T(1024)S(1)}) all-reduce(f32[2048]{0:T(1024)S(1)} %get-tuple-element.25, f32[2048]{0:T(1024)S(1)} %get-tuple-element.24), channel_id=1, replica_groups=mesh['groups'=2,'feat'=4,'dp'=4] {'dp'}, use_global_device_ids=true, to_apply=%region_3.0 | all-reduce | flops 4096 | bytes 32768 | tf_op jit(solution)/shard_map/psum | solution.py:49
  21.4 16.7 %convolution_convert_fusion = bf16[256,8192]{1,0:T(8,128)(2,1)} fusion(bf16[2048,8192]{1,0:T(8,128)(2,1)} %param.7, bf16[256,2048]{1,0:T(8,128)(2,1)} %param.4, f32[2048]{0:T(1024)} %param.6, f32[2048]{0:T(1024)} %param.5, f32[2048]{0:T(1024)S(1)} %get-tuple-element.39, f32[2048]{0:T(1024)S(1)} %get-tuple-element.38), kind=kOutput, calls=%fused_computation | convolution fusion | flops 8595701760 | bytes 38830080 | tf_op jit(solution)/shard_map/dot_general | solution.py:54
  38.1 0.0 reduce-scatter.2.cloned.1.call-update
  38.2 0.0 all-gather.5.cloned.1.call-start
  38.2 77.2 %reduce-scatter.2.cloned.1.call-done = bf16[256,2048]{1,0:T(8,128)(2,1)} async-done(((bf16[256,8192]{1,0:T(8,128)(2,1)}), bf16[256,2048]{1,0:T(8,128)(2,1)}) %reduce-scatter.2.cloned.1.call-update) | async-done | bytes 1048592 | tf_op jit(solution)/shard_map/reduce_scatter | solution.py:55
  115.4 1.4 convert_reduce_fusion.1
  116.8 7.0 %psum.30 = f32[2048]{0:T(1024)S(1)} all-reduce(f32[2048]{0:T(1024)S(1)} %convert_reduce_fusion.1), channel_id=1, replica_groups=mesh['groups'=2,'feat'=4,'dp'=4] {'dp'}, use_global_device_ids=true, to_apply=%region_6.0 | all-reduce | flops 2048 | bytes 16384 | tf_op jit(solution)/shard_map/psum | solution.py:56
  123.8 1.4 fusion.17
  125.3 1.1 fusion.37
  126.4 0.0 all-gather.5.cloned.1.call-update
  126.5 0.0 all-gather.3.cloned.1.call-start
  126.5 0.6 collective-permute-start
  127.1 23.2 %collective-permute-done = bf16[256,2048]{1,0:T(8,128)(2,1)S(1)} collective-permute-done((bf16[256,2048]{1,0:T(8,128)(2,1)S(1)}, bf16[256,2048]{1,0:T(8,128)(2,1)S(1)}, u32[]{:S(2)}, u32[]{:S(2)}) %collective-permute-start) | collective-permute-done | bytes 1048608 | tf_op jit(solution)/shard_map/ppermute | solution.py:9
  150.3 1.6 pad_maximum_fusion.1
  151.9 0.0 collective-permute-start.1
  151.9 0.0 all-gather.3.cloned.1.call-update
  151.9 0.0 all-reduce.3.cloned.1.call-start
  152.0 4.4 %collective-permute-done.1 = bf16[512,2048]{1,0:T(8,128)(2,1)} collective-permute-done((bf16[512,2048]{1,0:T(8,128)(2,1)}, bf16[512,2048]{1,0:T(8,128)(2,1)}, u32[]{:S(2)}, u32[]{:S(2)}) %collective-permute-start.1) | collective-permute-done | bytes 2097184 | tf_op jit(solution)/shard_map/ppermute | solution.py:9
  156.4 2.2 multiply_reduce_fusion
  158.6 13.8 %all_gather.11 = f32[8192]{0:T(1024)S(1)} all-gather(f32[2048]{0:T(1024)S(1)} %multiply_add_fusion), channel_id=1, replica_groups=mesh['groups'=2,'feat'=4,'dp'=4] {'feat'}, dimensions={0}, use_global_device_ids=true | all-gather | bytes 40960 | tf_op jit(solution)/shard_map/all_gather | solution.py:71
  172.4 0.0 copy-done.2
  172.4 3.9 %fusion.36 = f32[256,1024]{1,0:T(8,128)} fusion(bf16[256,2048]{1,0:T(8,128)(2,1)S(1)} %fusion.17, bf16[512,2048]{1,0:T(8,128)(2,1)} %collective-permute-done.1, bf16[256,2048]{1,0:T(8,128)(2,1)S(1)} %collective-permute-done), kind=kOutput, calls=%fused_computation.66 | convolution fusion | flops 1086324736 | bytes 5242880 | tf_op jit(solution)/shard_map/dot_general | solution.py:63
  176.3 0.0 all-reduce.3.cloned.1.call-update
  176.3 2.9 constant_dynamic-slice_fusion.3
  179.2 39.7 %all-gather.3.cloned.1.call-done = bf16[128,8192]{1,0:T(8,128)(2,1)} async-done(((bf16[128,2048]{1,0:T(8,128)(2,1)}), bf16[128,8192]{1,0:T(8,128)(2,1)}) %all-gather.3.cloned.1.call-update) | async-done | bytes 2097168 | tf_op jit(solution)/shard_map/all_gather | solution.py:59
  218.9 3.0 constant_dynamic-slice_fusion
  222.0 1.5 collective-permute-start.2
  223.4 0.6 collective-permute-start.3
  224.0 0.0 collective-permute-start.4
  224.0 0.5 collective-permute-start.5
  224.5 1.1 collective-permute-start.6
  225.6 0.0 copy-done.1
  225.6 1.5 constant_dynamic-update-slice_fusion.8
  227.1 0.0 copy-done
  227.1 1.4 constant_dynamic-update-slice_fusion.7
  228.5 17.0 %fusion.38 = f32[256,2048]{1,0:T(8,128)} fusion(bf16[256,8192]{1,0:T(8,128)(2,1)} %constant_dynamic-update-slice_fusion.7, bf16[2048,8192]{1,0:T(8,128)(2,1)} %param.7), kind=kOutput, calls=%fused_computation.68 | convolution fusion | flops 8589934592 | bytes 39845888 | tf_op jit(solution)/shard_map/dot_general | solution.py:82
  245.6 17.1 %fusion = f32[256,2048]{1,0:T(8,128)} fusion(bf16[2048,8192]{1,0:T(8,128)(2,1)} %param.7, bf16[256,8192]{1,0:T(8,128)(2,1)} %constant_dynamic-update-slice_fusion.7, f32[8192]{0:T(1024)S(1)} %all_gather.11), kind=kOutput, calls=%fused_computation.4 | convolution fusion | flops 8596226048 | bytes 39878656 | tf_op jit(solution)/shard_map/dot_general | solution.py:85
  262.6 0.0 copy-done.4
  262.7 0.8 constant_dynamic-update-slice_fusion.6
  263.5 1.7 convert_element_type.40
  265.2 0.0 collective-permute-done.2
  265.2 0.7 collective-permute-start.8
  265.9 1.9 constant_dynamic-update-slice_fusion.5
  267.8 0.0 collective-permute-done.3
  267.8 0.0 copy-done.5
  267.8 1.2 collective-permute-start.7
  269.0 1.9 constant_dynamic-update-slice_fusion.4
  270.9 0.0 collective-permute-done.4
  270.9 2.0 constant_dynamic-update-slice_fusion.3
  272.9 0.0 collective-permute-done.5
  272.9 1.9 constant_dynamic-update-slice_fusion.2
  274.8 0.0 collective-permute-done.6
  274.8 1.9 constant_dynamic-update-slice_fusion.1
  276.7 14.6 %collective-permute-done.8 = bf16[256,2048]{1,0:T(8,128)(2,1)S(1)} collective-permute-done((bf16[256,2048]{1,0:T(8,128)(2,1)S(1)}, bf16[256,2048]{1,0:T(8,128)(2,1)S(1)}, u32[]{:S(2)}, u32[]{:S(2)}) %collective-permute-start.8) | collective-permute-done | bytes 1048608 | tf_op jit(solution)/shard_map/ppermute | solution.py:9
  291.3 1.4 pad_maximum_fusion.2
  292.7 0.0 collective-permute-start.9
  292.7 9.0 %collective-permute-done.7 = bf16[128,2048]{1,0:T(8,128)(2,1)S(1)} collective-permute-done((bf16[128,2048]{1,0:T(8,128)(2,1)S(1)}, bf16[128,2048]{1,0:T(8,128)(2,1)S(1)}, u32[]{:S(2)}, u32[]{:S(2)}) %collective-permute-start.7) | collective-permute-done | bytes 524320 | tf_op jit(solution)/shard_map/ppermute | solution.py:9
  301.7 0.0 copy-done.6
  301.7 13.9 %convolution_multiply_fusion = f32[2048,2048]{1,0:T(8,128)} fusion(bf16[1024,2048]{1,0:T(8,128)(2,1)S(1)} %constant_dynamic-update-slice_fusion, bf16[512,2048]{1,0:T(8,128)(2,1)} %collective-permute-done.1, bf16[256,2048]{1,0:T(8,128)(2,1)S(1)} %copy-done.3, bf16[256,2048]{1,0:T(8,128)(2,1)S(1)} %fusion.17), kind=kOutput, calls=%fused_computation.1 | convolution fusion | flops 8606711808 | bytes 25165824 | tf_op jit(solution)/shard_map/dot_general | solution.py:88
  315.7 1.3 select_reduce_fusion
  317.0 0.0 collective-permute-done.9
  317.0 5.5 %fusion.14 = bf16[256,2048]{1,0:T(8,128)(2,1)} fusion(f32[256,2048]{1,0:T(8,128)} %fusion, bf16[512,2048]{1,0:T(8,128)(2,1)} %collective-permute-done.9, bf16[256,2048]{1,0:T(8,128)(2,1)S(1)} %collective-permute-done.8, bf16[256,2048]{1,0:T(8,128)(2,1)S(1)} %convert_element_type.40, f32[256,2048]{1,0:T(8,128)} %fusion.38, f32[256]{0:T(256)S(1)} %select_reduce_fusion, ...), kind=kOutput, calls=%fused_computation.20 | convolution fusion | flops 1089470464 | bytes 10486784 | tf_op jit(solution)/shard_map/dot_general | solution.py:99
  (14 shorter events, 0.1 us)
Async XLA Ops:
  7.2 108.3 %reduce-scatter.2.cloned.1.call-start = ((), (), s32[]{:S(2)}) async-start(), calls=%async_computation.1 | async-start | bytes 5242880 | tf_op jit(solution)/shard_map/reduce_scatter | solution.py:55
  38.2 138.1 %all-gather.5.cloned.1.call-start = ((), (), s32[]{:S(2)}) async-start(), calls=%async_computation.4 | async-start | bytes 2621440 | tf_op jit(solution)/shard_map/all_gather | solution.py:60
  126.5 92.5 %all-gather.3.cloned.1.call-start = ((), (), s32[]{:S(2)}) async-start(), calls=%async_computation.3 | async-start | bytes 2621440 | tf_op jit(solution)/shard_map/all_gather | solution.py:59
  126.5 23.8 %collective-permute-start = (bf16[256,2048]{1,0:T(8,128)(2,1)S(1)}, bf16[256,2048]{1,0:T(8,128)(2,1)S(1)}, u32[]{:S(2)}, u32[]{:S(2)}) collective-permute-start(bf16[256,2048]{1,0:T(8,128)(2,1)S(1)} %fusion.17), channel_id=1, source_target_pairs={{0,2},{1,3},{2,0},{3,1},{4,6},{5,7},{6,4},{7,5},{8,10},{9,11},{10,... | collective-permute-start | bytes 3145736 | tf_op jit(solution)/shard_map/ppermute | solution.py:9
  150.3 22.2 %copy-start.2 = (bf16[256,2048]{1,0:T(8,128)(2,1)}, bf16[256,2048]{1,0:T(8,128)(2,1)S(1)}, u32[]{:S(2)}) copy-start(bf16[256,2048]{1,0:T(8,128)(2,1)S(1)} %collective-permute-done) | copy-start | bytes 3145732
  151.9 4.5 %collective-permute-start.1 = (bf16[512,2048]{1,0:T(8,128)(2,1)}, bf16[512,2048]{1,0:T(8,128)(2,1)}, u32[]{:S(2)}, u32[]{:S(2)}) collective-permute-start(bf16[512,2048]{1,0:T(8,128)(2,1)} %pad_maximum_fusion.1), channel_id=1, source_target_pairs={{0,1},{1,0},{2,3},{3,2},{4,5},{5,4},{6,7},{7,6},{8,9},{9,8},{10,11... | collective-permute-start | bytes 6291464 | tf_op jit(solution)/shard_map/ppermute | solution.py:9
  151.9 163.7 %all-reduce.3.cloned.1.call-start = ((), (), s32[]{:S(2)}) async-start(), calls=%async_computation.2 | async-start | bytes 2097152 | tf_op jit(solution)/shard_map/psum | solution.py:76
  179.2 47.8 %copy-start = (bf16[128,8192]{1,0:T(8,128)(2,1)S(1)}, bf16[128,8192]{1,0:T(8,128)(2,1)}, u32[]{:S(2)}) copy-start(bf16[128,8192]{1,0:T(8,128)(2,1)} %all-gather.5.cloned.1.call-done) | copy-start | bytes 6291460
  218.9 6.6 %copy-start.1 = (bf16[128,8192]{1,0:T(8,128)(2,1)S(1)}, bf16[128,8192]{1,0:T(8,128)(2,1)}, u32[]{:S(2)}) copy-start(bf16[128,8192]{1,0:T(8,128)(2,1)} %all-gather.3.cloned.1.call-done) | copy-start | bytes 6291460
  222.0 43.3 %collective-permute-start.2 = (bf16[128,2048]{1,0:T(8,128)(2,1)}, bf16[128,2048]{1,0:T(8,128)(2,1)}, u32[]{:S(2)}, u32[]{:S(2)}) collective-permute-start(bf16[128,2048]{1,0:T(8,128)(2,1)} %get-tuple-element.30), channel_id=1, source_target_pairs={{0,2},{1,3},{2,0},{3,1},{4,6},{5,7},{6,4},{7,5},{8,10},{9,11},{10,... | collective-permute-start | bytes 1572872 | tf_op jit(solution)/shard_map/ppermute | solution.py:9
  223.4 44.4 %collective-permute-start.3 = (bf16[128,2048]{1,0:T(8,128)(2,1)}, bf16[128,2048]{1,0:T(8,128)(2,1)}, u32[]{:S(2)}, u32[]{:S(2)}) collective-permute-start(bf16[128,2048]{1,0:T(8,128)(2,1)} %get-tuple-element.15), channel_id=1, source_target_pairs={{0,2},{1,3},{2,0},{3,1},{4,6},{5,7},{6,4},{7,5},{8,10},{9,11},{10,... | collective-permute-start | bytes 1572872 | tf_op jit(solution)/shard_map/ppermute | solution.py:9
  224.0 46.9 %collective-permute-start.4 = (bf16[128,2048]{1,0:T(8,128)(2,1)}, bf16[128,2048]{1,0:T(8,128)(2,1)}, u32[]{:S(2)}, u32[]{:S(2)}) collective-permute-start(bf16[128,2048]{1,0:T(8,128)(2,1)} %get-tuple-element.29), channel_id=1, source_target_pairs={{0,1},{1,0},{2,3},{3,2},{4,5},{5,4},{6,7},{7,6},{8,9},{9,8},{10,11... | collective-permute-start | bytes 1572872 | tf_op jit(solution)/shard_map/ppermute | solution.py:9
  224.0 48.9 %collective-permute-start.5 = (bf16[128,2048]{1,0:T(8,128)(2,1)}, bf16[128,2048]{1,0:T(8,128)(2,1)}, u32[]{:S(2)}, u32[]{:S(2)}) collective-permute-start(bf16[128,2048]{1,0:T(8,128)(2,1)} %get-tuple-element.16), channel_id=1, source_target_pairs={{0,1},{1,0},{2,3},{3,2},{4,5},{5,4},{6,7},{7,6},{8,9},{9,8},{10,11... | collective-permute-start | bytes 1572872 | tf_op jit(solution)/shard_map/ppermute | solution.py:9
  224.5 50.3 %collective-permute-start.6 = (bf16[128,2048]{1,0:T(8,128)(2,1)}, bf16[128,2048]{1,0:T(8,128)(2,1)}, u32[]{:S(2)}, u32[]{:S(2)}) collective-permute-start(bf16[128,2048]{1,0:T(8,128)(2,1)} %get-tuple-element.28), channel_id=1, source_target_pairs={{0,3},{1,2},{2,1},{3,0},{4,7},{5,6},{6,5},{7,4},{8,11},{9,10},{10,... | collective-permute-start | bytes 1572872 | tf_op jit(solution)/shard_map/ppermute | solution.py:9
  245.6 17.1 %copy-start.4 = (bf16[128,2048]{1,0:T(8,128)(2,1)S(1)}, bf16[128,2048]{1,0:T(8,128)(2,1)}, u32[]{:S(2)}) copy-start(bf16[128,2048]{1,0:T(8,128)(2,1)} %get-tuple-element.14) | copy-start | bytes 1572868
  262.6 5.2 %copy-start.5 = (bf16[128,2048]{1,0:T(8,128)(2,1)S(1)}, bf16[128,2048]{1,0:T(8,128)(2,1)}, u32[]{:S(2)}) copy-start(bf16[128,2048]{1,0:T(8,128)(2,1)} %get-tuple-element.17) | copy-start | bytes 1572868
  265.2 26.0 %collective-permute-start.8 = (bf16[256,2048]{1,0:T(8,128)(2,1)S(1)}, bf16[256,2048]{1,0:T(8,128)(2,1)S(1)}, u32[]{:S(2)}, u32[]{:S(2)}) collective-permute-start(bf16[256,2048]{1,0:T(8,128)(2,1)S(1)} %convert_element_type.40), channel_id=1, source_target_pairs={{0,2},{1,3},{2,0},{3,1},{4,6},{5,7},{6,4},{7,5},{8,10},{9,11},{10,... | collective-permute-start | bytes 3145736 | tf_op jit(solution)/shard_map/ppermute | solution.py:9
  267.8 33.9 %collective-permute-start.7 = (bf16[128,2048]{1,0:T(8,128)(2,1)S(1)}, bf16[128,2048]{1,0:T(8,128)(2,1)S(1)}, u32[]{:S(2)}, u32[]{:S(2)}) collective-permute-start(bf16[128,2048]{1,0:T(8,128)(2,1)S(1)} %copy-done.5), channel_id=1, source_target_pairs={{0,3},{1,2},{2,1},{3,0},{4,7},{5,6},{6,5},{7,4},{8,11},{9,10},{10,... | collective-permute-start | bytes 1572872 | tf_op jit(solution)/shard_map/ppermute | solution.py:9
  270.9 30.8 %copy-start.3 = (bf16[256,2048]{1,0:T(8,128)(2,1)S(1)}, bf16[256,2048]{1,0:T(8,128)(2,1)}, u32[]{:S(2)}) copy-start(bf16[256,2048]{1,0:T(8,128)(2,1)} %copy-done.2) | copy-start | bytes 3145732
  276.7 25.0 %copy-start.6 = (bf16[1024,2048]{1,0:T(8,128)(2,1)S(1)}, bf16[1024,2048]{1,0:T(8,128)(2,1)}, u32[]{:S(2)}) copy-start(bf16[1024,2048]{1,0:T(8,128)(2,1)} %constant_dynamic-update-slice_fusion.1) | copy-start | bytes 12582916
  292.7 24.3 %collective-permute-start.9 = (bf16[512,2048]{1,0:T(8,128)(2,1)}, bf16[512,2048]{1,0:T(8,128)(2,1)}, u32[]{:S(2)}, u32[]{:S(2)}) collective-permute-start(bf16[512,2048]{1,0:T(8,128)(2,1)} %pad_maximum_fusion.2), channel_id=1, source_target_pairs={{0,1},{1,0},{2,3},{3,2},{4,5},{5,4},{6,7},{7,6},{8,9},{9,8},{10,11... | collective-permute-start | bytes 6291464 | tf_op jit(solution)/shard_map/ppermute | solution.py:9
Sparse Core Ops, SparseCore 0:
  38.3 77.0 reduce-scatter.1
  126.6 45.9 all-gather.4
  174.2 44.6 all-gather.2
  221.3 50.5 all-reduce.2

commit v4 on v2

--- a/solution.py
+++ b/solution.py
@@ -37,7 +37,7 @@
 
 def exchange(blocks):
     order = block_order(lax.axis_size("dp"))
-    return jnp.concatenate([swap(b, o) if o else b for b, o in zip(blocks, order)], 0)
+    return [swap(b, o) if o else b for b, o in zip(blocks, order)]
 
 
 def shards(features, bn_gain, bn_shift, weight):
@@ -72,11 +72,13 @@
     cent_full, factor, _ = lax.optimization_barrier((cent_full, factor, gram))
     gram = lax.psum(gram, "feat")
     cent_full, cuts = lax.optimization_barrier((cent_full, column_blocks(cent_full)))
-    cent_x = exchange(cuts)
+    blocks = exchange(cuts)
     scaled = (cent_full.astype(jnp.float32) * factor).astype(jnp.bfloat16)
     dims = (((1,), (1,)), ((), ()))
+    direct = lax.dot_general(scaled, weight, dims, preferred_element_type=jnp.float32)
+    cent_full, direct, gram, blocks = lax.optimization_barrier((cent_full, direct, gram, blocks))
+    cent_x = jnp.concatenate(blocks, 0)
     through = lax.dot_general(cent_full, weight, dims, preferred_element_type=jnp.float32)
-    direct = lax.dot_general(scaled, weight, dims, preferred_element_type=jnp.float32)
     through_all = gather_rows(through.astype(jnp.bfloat16))
 
     covariance = lax.dot_general(

time: 328 us -> 329 us (level)
  waiting for transfers between devices: 179 us -> 187 us
  matrix products: 76.1 us -> 72.2 us
    psum x1, waiting for transfers between devices: 0.01 us -> 29.7 us  [shards(): gram = lax.psum(gram, 'feat')]
    ppermute x7, waiting for transfers between devices: 73.9 us -> 51.7 us  [swap(): return lax.ppermute(value, 'dp', [(i, i ^ distance) for i in range(count)])]
    dot_general x1, matrix products: 6.08 us -> 2.35 us  [shards(): jnp.dot(rest, through_all, preferred_element_type=jnp.float32)]
  transfers between devices with their start and end apart: 10 -> 10, of which waited for: 7 -> 6; matrix products, arithmetic and copies ran while one was open for 14% -> 14% of each run, Pallas kernels for 0% -> 0%
where the time goes in v4:
time: 329 us; the launch traced here: 328 us
  waiting for transfers between devices  187 us (57%)
  matrix products  72.2 us (22%)
  blocking collectives  35.1 us (11%)
  between operations  13.9 us (4%)
  other arithmetic  11.9 us (4%)
  starting transfers between devices  4.42 us (1%)
  local copies, waits for them, and re-layouts  3.99 us (1%)
    reduce_scatter x1, waiting for transfers between devices, shards(): lax.psum_scatter(partial_value, 'feat', scatter_dimension=1, tiled=True)  77.2 us
    ppermute x7, waiting for transfers between devices, swap(): return lax.ppermute(value, 'dp', [(i, i ^ distance) for i in range(count)])  51.7 us
    psum x1, waiting for transfers between devices, shards(): gram = lax.psum(gram, 'feat')  29.7 us
    all_gather x1, waiting for transfers between devices, shards(): cent_full = lax.all_gather(centered, 'feat', axis=1, tiled=True)  28 us
    dot_general x1, matrix products, shards(): lax.dot_general(cent_full, weight, dims, preferred_element_type=jnp.float32)  17.4 us
    dot_general x1, matrix products, shards(): lax.dot_general(scaled, weight, dims, preferred_element_type=jnp.float32)  17 us
    dot_general x1, matrix products, shards(): jnp.dot(activated, weight, preferred_element_type=jnp.float32)  16.7 us
    all_gather x1, blocking collectives, shards(): lax.all_gather(4.0 * scale_up * proj_var + 25.0 * scale_up * active, 'fea...  15.5 us
  transfers between devices with their start and end apart: 10, of which 6 were waited for; matrix products, arithmetic and copies ran while one was open for 14% of the time, Pallas kernels for 0%

profile of v4, /device:TPU:0, one launch (start us, length us, event | category | flops | bytes accessed | tf_op | source)
XLA Modules:
  0.0 328.2 jit_solution(4533079367253489197)
XLA Ops:
  7.2 0.0 reduce-scatter.2.cloned.1.call-start
  7.2 1.5 convert_reduce_fusion
  8.7 12.7 %all-reduce = (f32[2048]{0:T(1024)S(1)}, f32[2048]{0:T(1024)S(1)}) all-reduce(f32[2048]{0:T(1024)S(1)} %get-tuple-element.35, f32[2048]{0:T(1024)S(1)} %get-tuple-element.34), channel_id=1, replica_groups=mesh['groups'=2,'feat'=4,'dp'=4] {'dp'}, use_global_device_ids=true, to_apply=%region_3.0 | all-reduce | flops 4096 | bytes 32768 | tf_op jit(solution)/shard_map/psum | solution.py:49
  21.4 16.7 %convolution_convert_fusion = bf16[256,8192]{1,0:T(8,128)(2,1)} fusion(bf16[2048,8192]{1,0:T(8,128)(2,1)} %param.7, bf16[256,2048]{1,0:T(8,128)(2,1)} %param.4, f32[2048]{0:T(1024)} %param.6, f32[2048]{0:T(1024)} %param.5, f32[2048]{0:T(1024)S(1)} %get-tuple-element.43, f32[2048]{0:T(1024)S(1)} %get-tuple-element.42), kind=kOutput, calls=%fused_computation | convolution fusion | flops 8595701760 | bytes 38830080 | tf_op jit(solution)/shard_map/dot_general | solution.py:54
  38.1 0.0 reduce-scatter.2.cloned.1.call-update
  38.2 0.0 all-gather.2.cloned.1.call-start
  38.2 77.2 %reduce-scatter.2.cloned.1.call-done = bf16[256,2048]{1,0:T(8,128)(2,1)} async-done(((bf16[256,8192]{1,0:T(8,128)(2,1)}), bf16[256,2048]{1,0:T(8,128)(2,1)}) %reduce-scatter.2.cloned.1.call-update) | async-done | bytes 1048592 | tf_op jit(solution)/shard_map/reduce_scatter | solution.py:55
  115.4 1.4 convert_reduce_fusion.1
  116.8 7.0 %psum.30 = f32[2048]{0:T(1024)S(1)} all-reduce(f32[2048]{0:T(1024)S(1)} %convert_reduce_fusion.1), channel_id=1, replica_groups=mesh['groups'=2,'feat'=4,'dp'=4] {'dp'}, use_global_device_ids=true, to_apply=%region_6.0 | all-reduce | flops 2048 | bytes 16384 | tf_op jit(solution)/shard_map/psum | solution.py:56
  123.8 2.4 fusion.24
  126.3 0.0 copy-start
  126.3 0.0 all-gather.2.cloned.1.call-update
  126.3 0.0 all-reduce.3.cloned.1.call-start
  126.3 0.6 collective-permute-start
  126.9 23.4 %collective-permute-done = bf16[256,2048]{1,0:T(8,128)(2,1)S(1)} collective-permute-done((bf16[256,2048]{1,0:T(8,128)(2,1)}, bf16[256,2048]{1,0:T(8,128)(2,1)S(1)}, u32[]{:S(2)}, u32[]{:S(2)}) %collective-permute-start) | collective-permute-done | bytes 1048608 | tf_op jit(solution)/shard_map/ppermute | solution.py:9
  150.3 2.8 pad_maximum_fusion.1
  153.1 0.0 collective-permute-start.1
  153.1 4.5 %collective-permute-done.1 = bf16[512,2048]{1,0:T(8,128)(2,1)} collective-permute-done((bf16[512,2048]{1,0:T(8,128)(2,1)}, bf16[512,2048]{1,0:T(8,128)(2,1)}, u32[]{:S(2)}, u32[]{:S(2)}) %collective-permute-start.1) | collective-permute-done | bytes 2097184 | tf_op jit(solution)/shard_map/ppermute | solution.py:9
  157.6 0.0 copy-done
  157.6 2.2 multiply_reduce_fusion
  159.8 15.5 %all_gather.7 = f32[8192]{0:T(1024)S(1)} all-gather(f32[2048]{0:T(1024)S(1)} %multiply_add_fusion), channel_id=1, replica_groups=mesh['groups'=2,'feat'=4,'dp'=4] {'feat'}, dimensions={0}, use_global_device_ids=true | all-gather | bytes 40960 | tf_op jit(solution)/shard_map/all_gather | solution.py:69
  175.3 4.0 %fusion.44 = f32[256,1024]{1,0:T(8,128)} fusion(bf16[256,2048]{1,0:T(8,128)(2,1)S(1)} %copy-done, bf16[512,2048]{1,0:T(8,128)(2,1)} %collective-permute-done.1, bf16[256,2048]{1,0:T(8,128)(2,1)S(1)} %collective-permute-done), kind=kOutput, calls=%fused_computation.61 | convolution fusion | flops 1086324736 | bytes 5242880 | tf_op jit(solution)/shard_map/dot_general | solution.py:61
  179.3 28.0 %all-gather.2.cloned.1.call-done = bf16[256,8192]{1,0:T(8,128)(2,1)} async-done(((bf16[256,2048]{1,0:T(8,128)(2,1)}), bf16[256,8192]{1,0:T(8,128)(2,1)}) %all-gather.2.cloned.1.call-update) | async-done | bytes 4194320 | tf_op jit(solution)/shard_map/all_gather | solution.py:58
  207.2 0.0 all-reduce.3.cloned.1.call-update
  207.2 4.0 %constant_dynamic-slice_fusion = (bf16[256,2048]{1,0:T(8,128)(2,1)}, bf16[256,2048]{1,0:T(8,128)(2,1)}, bf16[256,2048]{1,0:T(8,128)(2,1)}, bf16[256,2048]{1,0:T(8,128)(2,1)S(1)}) fusion(bf16[256,8192]{1,0:T(8,128)(2,1)} %all-gather.2.cloned.1.call-done, s32[]{:T(128)S(6)} %select_n.28, s32[]{:T(128)S(6)} %select_n.27, s32[]{:T(128)S(6)} %select_n.26, ...), kind=kLoop, calls=%fused_computation.52 | loop fusion | bytes 8388624 | tf_op jit(solution)/shard_map/dynamic_slice | solution.py:34
  211.2 1.5 collective-permute-start.2
  212.7 0.0 collective-permute-start.3
  212.7 0.7 collective-permute-start.4
  213.3 17.0 %fusion = f32[256,2048]{1,0:T(8,128)} fusion(bf16[2048,8192]{1,0:T(8,128)(2,1)} %param.7, bf16[256,8192]{1,0:T(8,128)(2,1)} %all-gather.2.cloned.1.call-done, f32[8192]{0:T(1024)S(1)} %all_gather.7), kind=kOutput, calls=%fused_computation.4 | convolution fusion | flops 8596226048 | bytes 39878656 | tf_op jit(solution)/shard_map/dot_general | solution.py:78
  230.4 29.7 %all-reduce.3.cloned.1.call-done = f32[256,1024]{1,0:T(8,128)} async-done(((f32[256,1024]{1,0:T(8,128)}), f32[256,1024]{1,0:T(8,128)}) %all-reduce.3.cloned.1.call-update) | async-done | bytes 1048592 | tf_op jit(solution)/shard_map/psum | solution.py:73
  260.1 0.0 collective-permute-done.2
  260.1 0.0 collective-permute-done.3
  260.1 0.0 collective-permute-done.4
  260.1 17.4 %fusion.45 = (bf16[256,2048]{1,0:T(8,128)(2,1)}, f32[256,2048]{1,0:T(8,128)}) fusion(bf16[256,8192]{1,0:T(8,128)(2,1)} %all-gather.2.cloned.1.call-done, bf16[2048,8192]{1,0:T(8,128)(2,1)} %param.7), kind=kOutput, calls=%fused_computation.62 | convolution fusion | flops 8590458880 | bytes 40894464 | tf_op jit(solution)/shard_map/dot_general | solution.py:81
  277.5 1.5 collective-permute-start.5
  278.9 23.9 %collective-permute-done.5 = bf16[256,2048]{1,0:T(8,128)(2,1)S(1)} collective-permute-done((bf16[256,2048]{1,0:T(8,128)(2,1)}, bf16[256,2048]{1,0:T(8,128)(2,1)S(1)}, u32[]{:S(2)}, u32[]{:S(2)}) %collective-permute-start.5) | collective-permute-done | bytes 1048608 | tf_op jit(solution)/shard_map/ppermute | solution.py:9
  302.8 1.5 pad_maximum_fusion.2
  304.2 0.0 copy-start.1
  304.3 0.0 copy-start.2
  304.3 0.0 copy-start.3
  304.3 0.0 copy-start.4
  304.3 0.1 collective-permute-start.6
  304.4 14.8 %convolution_multiply_fusion = f32[2048,2048]{1,0:T(8,128)} fusion(bf16[256,2048]{1,0:T(8,128)(2,1)} %collective-permute-done.4, bf16[256,2048]{1,0:T(8,128)(2,1)} %collective-permute-done.3, bf16[256,2048]{1,0:T(8,128)(2,1)} %collective-permute-done.2, bf16[256,2048]{1,0:T(8,128)(2,1)S(1)} %get-tuple-element.26, ...), kind=kOutput, calls=%fused_computation.1 | convolution fusion | flops 8623489024 | bytes 25165824 | tf_op jit(solution)/shard_map/dot_general | solution.py:84
  319.2 0.0 copy-done.1
  319.2 0.1 select_reduce_fusion
  319.3 0.0 collective-permute-done.6
  319.3 0.0 copy-done.2
  319.3 0.0 copy-done.3
  319.3 0.0 copy-done.4
  319.3 2.4 fusion.21
  (3 shorter events, 0.0 us)
Async XLA Ops:
  7.2 108.3 %reduce-scatter.2.cloned.1.call-start = ((), (), s32[]{:S(2)}) async-start(), calls=%async_computation.1 | async-start | bytes 5242880 | tf_op jit(solution)/shard_map/reduce_scatter | solution.py:55
  38.2 169.0 %all-gather.2.cloned.1.call-start = ((), (), s32[]{:S(2)}) async-start(), calls=%async_computation.2 | async-start | bytes 5242880 | tf_op jit(solution)/shard_map/all_gather | solution.py:58
  126.3 31.4 %copy-start = (bf16[256,2048]{1,0:T(8,128)(2,1)S(1)}, bf16[256,2048]{1,0:T(8,128)(2,1)}, u32[]{:S(2)}) copy-start(bf16[256,2048]{1,0:T(8,128)(2,1)} %fusion.24) | copy-start | bytes 3145732
  126.3 133.8 %all-reduce.3.cloned.1.call-start = ((), (), s32[]{:S(2)}) async-start(), calls=%async_computation.3 | async-start | bytes 2097152 | tf_op jit(solution)/shard_map/psum | solution.py:73
  126.3 24.0 %collective-permute-start = (bf16[256,2048]{1,0:T(8,128)(2,1)}, bf16[256,2048]{1,0:T(8,128)(2,1)S(1)}, u32[]{:S(2)}, u32[]{:S(2)}) collective-permute-start(bf16[256,2048]{1,0:T(8,128)(2,1)} %fusion.24), channel_id=1, source_target_pairs={{0,2},{1,3},{2,0},{3,1},{4,6},{5,7},{6,4},{7,5},{8,10},{9,11},{10,... | collective-permute-start | bytes 3145736 | tf_op jit(solution)/shard_map/ppermute | solution.py:9
  153.1 4.5 %collective-permute-start.1 = (bf16[512,2048]{1,0:T(8,128)(2,1)}, bf16[512,2048]{1,0:T(8,128)(2,1)}, u32[]{:S(2)}, u32[]{:S(2)}) collective-permute-start(bf16[512,2048]{1,0:T(8,128)(2,1)} %pad_maximum_fusion.1), channel_id=1, source_target_pairs={{0,1},{1,0},{2,3},{3,2},{4,5},{5,4},{6,7},{7,6},{8,9},{9,8},{10,11... | collective-permute-start | bytes 6291464 | tf_op jit(solution)/shard_map/ppermute | solution.py:9
  211.2 48.9 %collective-permute-start.2 = (bf16[256,2048]{1,0:T(8,128)(2,1)}, bf16[256,2048]{1,0:T(8,128)(2,1)}, u32[]{:S(2)}, u32[]{:S(2)}) collective-permute-start(bf16[256,2048]{1,0:T(8,128)(2,1)} %get-tuple-element.22), channel_id=1, source_target_pairs={{0,2},{1,3},{2,0},{3,1},{4,6},{5,7},{6,4},{7,5},{8,10},{9,11},{10,... | collective-permute-start | bytes 3145736 | tf_op jit(solution)/shard_map/ppermute | solution.py:9
  212.7 47.4 %collective-permute-start.3 = (bf16[256,2048]{1,0:T(8,128)(2,1)}, bf16[256,2048]{1,0:T(8,128)(2,1)}, u32[]{:S(2)}, u32[]{:S(2)}) collective-permute-start(bf16[256,2048]{1,0:T(8,128)(2,1)} %get-tuple-element.23), channel_id=1, source_target_pairs={{0,1},{1,0},{2,3},{3,2},{4,5},{5,4},{6,7},{7,6},{8,9},{9,8},{10,11... | collective-permute-start | bytes 3145736 | tf_op jit(solution)/shard_map/ppermute | solution.py:9
  212.7 47.4 %collective-permute-start.4 = (bf16[256,2048]{1,0:T(8,128)(2,1)}, bf16[256,2048]{1,0:T(8,128)(2,1)}, u32[]{:S(2)}, u32[]{:S(2)}) collective-permute-start(bf16[256,2048]{1,0:T(8,128)(2,1)} %get-tuple-element.24), channel_id=1, source_target_pairs={{0,3},{1,2},{2,1},{3,0},{4,7},{5,6},{6,5},{7,4},{8,11},{9,10},{10,... | collective-permute-start | bytes 3145736 | tf_op jit(solution)/shard_map/ppermute | solution.py:9
  277.5 25.3 %collective-permute-start.5 = (bf16[256,2048]{1,0:T(8,128)(2,1)}, bf16[256,2048]{1,0:T(8,128)(2,1)S(1)}, u32[]{:S(2)}, u32[]{:S(2)}) collective-permute-start(bf16[256,2048]{1,0:T(8,128)(2,1)} %get-tuple-element.44), channel_id=1, source_target_pairs={{0,2},{1,3},{2,0},{3,1},{4,6},{5,7},{6,4},{7,5},{8,10},{9,11},{10,... | collective-permute-start | bytes 3145736 | tf_op jit(solution)/shard_map/ppermute | solution.py:9
  304.2 14.9 %copy-start.1 = (f32[256,1024]{1,0:T(8,128)S(1)}, f32[256,1024]{1,0:T(8,128)}, u32[]{:S(2)}) copy-start(f32[256,1024]{1,0:T(8,128)} %all-reduce.3.cloned.1.call-done) | copy-start | bytes 3145732
  304.3 15.1 %copy-start.2 = (bf16[256,2048]{1,0:T(8,128)(2,1)S(1)}, bf16[256,2048]{1,0:T(8,128)(2,1)}, u32[]{:S(2)}) copy-start(bf16[256,2048]{1,0:T(8,128)(2,1)} %get-tuple-element.44) | copy-start | bytes 3145732
  304.3 15.1 %copy-start.3 = (f32[256,2048]{1,0:T(8,128)S(1)}, f32[256,2048]{1,0:T(8,128)}, u32[]{:S(2)}) copy-start(f32[256,2048]{1,0:T(8,128)} %fusion) | copy-start | bytes 6291460
  304.3 15.1 %copy-start.4 = (f32[256,2048]{1,0:T(8,128)S(1)}, f32[256,2048]{1,0:T(8,128)}, u32[]{:S(2)}) copy-start(f32[256,2048]{1,0:T(8,128)} %get-tuple-element.45) | copy-start | bytes 6291460
  304.3 15.0 %collective-permute-start.6 = (bf16[512,2048]{1,0:T(8,128)(2,1)S(1)}, bf16[512,2048]{1,0:T(8,128)(2,1)S(1)}, u32[]{:S(2)}, u32[]{:S(2)}) collective-permute-start(bf16[512,2048]{1,0:T(8,128)(2,1)S(1)} %pad_maximum_fusion.2), channel_id=1, source_target_pairs={{0,1},{1,0},{2,3},{3,2},{4,5},{5,4},{6,7},{7,6},{8,9},{9,8},{10,11... | collective-permute-start | bytes 6291464 | tf_op jit(solution)/shard_map/ppermute | solution.py:9
Sparse Core Ops, SparseCore 0:
  38.3 77.0 reduce-scatter.1
  126.4 80.7 all-gather.1
  209.7 50.3 all-reduce.2
